TPU v7x, 512 devices: a whole 4x8x8 slice. The times are simulated.
512 devices in a mesh: dp: 64 (over z, y), mp: 8 (over x, core).
Axes of the slice: x: 4, y: 8, z: 8, core: 2. Of those that a mesh axis runs over, the one named last changes fastest.
Arguments:
- inputs: bfloat16 [32768, 1024], P('dp', 'mp'), may hold values from -6 to 6
- out_grads: bfloat16 [32768, 8192], P('dp', 'mp'), may hold values from -0.03125 to 0.03125
- sketch: float32 [8, 1024, 256], P('mp', 'dp'), may hold values from -6 to 6
Outputs:
- update: float32 [8, 1024, 1024], P('mp', None, 'dp')
- new_sketch: float32 [8, 1024, 256], P('mp', 'dp')
All inputs are finite; a program needn't handle non-finite values.
Results may differ from a plain program's by a relative error of at most 0.00045.
Values may be sent and summed in bfloat16 or wider, within the bound.
No kernel may reach another device: no remote copies, remote signals or barrier semaphores. Data moves between devices by JAX's collectives and lax.ppermute only.
A program may use at most 64 MiB of HBM per device.

v0:
```python
import jax
import jax.numpy as jnp
from jax import lax
from jax.sharding import PartitionSpec as P

NS_ITERS = 8


def matmul(left, right):
    return jnp.dot(left, right, precision=lax.Precision.HIGHEST, preferred_element_type=jnp.float32)


def inner_rows(left, right):
    return lax.dot_general(
        left,
        right,
        (((0,), (0,)), ((), ())),
        precision=lax.Precision.HIGHEST,
        preferred_element_type=jnp.float32,
    )


def root_pair(matrix):
    order = matrix.shape[0]
    ident = jnp.eye(order, dtype=jnp.float32)
    scale = jnp.trace(matrix)
    ymat = matrix / scale
    zmat = ident
    for step in range(NS_ITERS):
        weight = 1.5 * ident - 0.5 * matmul(zmat, ymat)
        ymat, zmat = (matmul(ymat, weight), matmul(weight, zmat))
    return (jnp.sqrt(scale) * ymat, zmat / jnp.sqrt(scale))


def finish(gram, ritz):
    rank = gram.shape[0]
    ident = jnp.eye(rank, dtype=jnp.float32)
    unused, cinv = root_pair(gram)
    hmat = matmul(matmul(cinv, ritz), cinv)
    eps = 0.1 * jnp.trace(hmat) / rank
    root, rinv = root_pair(hmat + eps * ident)
    return (cinv, root, jnp.sqrt(eps) * rinv - ident)


def per_device(inputs, out_grads, sketch):
    whole = lax.all_gather(inputs, "mp", axis=1, tiled=True)
    local_sketch = sketch[0]
    grad_part = lax.psum_scatter(
        lax.dot_general(
            whole, out_grads, (((0,), (0,)), ((), ())), preferred_element_type=jnp.float32
        ),
        "dp",
        scatter_dimension=0,
        tiled=True,
    )
    sgram, gsk = lax.psum(
        (inner_rows(local_sketch, local_sketch), inner_rows(grad_part, local_sketch)), "dp"
    )
    power = 0.95 * matmul(local_sketch, sgram) + matmul(grad_part, gsk)
    gram, spow, gpow = lax.psum(
        (inner_rows(power, power), inner_rows(local_sketch, power), inner_rows(grad_part, power)),
        "dp",
    )
    ritz = 0.95 * matmul(spow.T, spow) + matmul(gpow.T, gpow)
    cinv, root, middle = finish(gram, ritz)
    basis_part = matmul(power, cinv)
    fresh = matmul(basis_part, root)
    basis_full = lax.all_gather(basis_part, "dp", axis=0, tiled=True)
    grad_cols = lax.all_to_all(grad_part, "dp", split_axis=1, concat_axis=0, tiled=True)
    coef = inner_rows(basis_full, grad_cols)
    update = grad_cols + matmul(basis_full, matmul(middle, coef))
    return (update[None], fresh[None])


def solution(mesh):
    in_specs = (P("dp", "mp"), P("dp", "mp"), P("mp", "dp", None))
    out_specs = (P("mp", None, "dp"), P("mp", "dp", None))
    return jax.shard_map(
        per_device, mesh=mesh, in_specs=in_specs, out_specs=out_specs, check_vma=False
    )
```

profile of v0, /device:TPU:1, one launch (start us, length us, event | category | flops | bytes accessed | tf_op | source)
XLA Modules:
  0.0 738.2 jit_solution(4637088035005196904)
XLA Ops:
  7.2 0.7 all-gather.3.cloned.1.call-update
  8.0 36.8 %all-gather.3.cloned.1.call-done = bf16[512,1024]{1,0:T(8,128)(2,1)} async-done(((bf16[512,128]{1,0:T(8,128)(2,1)}), bf16[512,1024]{1,0:T(8,128)(2,1)}) %all-gather.3.cloned.1.call-update) | async-done | bytes 1048592 | tf_op jit(solution)/shard_map/all_gather | solution.py:46
  44.7 4.4 fusion.20
  49.3 1.1 fusion.16
  50.4 242.1 %reduce-scatter.2.cloned.1.call-done = f32[16,1024]{1,0:T(8,128)} async-done(((f32[1024,1024]{1,0:T(8,128)}), f32[16,1024]{1,0:T(8,128)}) %reduce-scatter.2.cloned.1.call-update) | async-done | bytes 65552 | tf_op jit(solution)/shard_map/reduce_scatter | solution.py:48
  292.4 3.0 fusion.13
  295.5 158.7 %all-reduce.7.cloned.1.call-done = (f32[256,256]{1,0:T(8,128)}, f32[1024,256]{1,0:T(8,128)}) async-done(((f32[256,256]{1,0:T(8,128)}, f32[1024,256]{1,0:T(8,128)}), (f32[256,256]{1,0:T(8,128)}, f32[1024,256]{1,0:T(8,128)})) %all-reduce.7.cloned.1.call-update) | async-done | bytes 1310736 | tf_op jit(solution)/shard_map/psum | solution.py:56
  454.1 1.2 fusion.4
  455.3 1.8 convolution_add_fusion.1
  457.1 1.1 convolution_bitcast_fusion
  458.3 1.1 fusion.21
  459.4 2.0 fusion.35
  462.3 18.5 %all_to_all.19 = f32[64,1,256]{2,1,0:T(1,128)S(1)} all-to-all(f32[64,1,256]{2,1,0:T(1,128)S(1)} %reshape.7), channel_id=1, replica_groups=mesh['dp'=64,'mp'=8] {'dp'}, dimensions={0} | all-to-all | bytes 131072 | tf_op jit(solution)/shard_map/all_to_all | solution.py:69
  480.8 0.5 broadcast.69
  481.3 0.8 reduce
  482.4 138.2 %all-reduce.5.cloned.1.call-done = (f32[256,256]{1,0:T(8,128)}, f32[1024,256]{1,0:T(8,128)}, f32[256,256]{0,1:T(8,128)}) async-done(((f32[256,256]{1,0:T(8,128)}, f32[1024,256]{1,0:T(8,128)}, f32[256,256]{0,1:T(8,128)}), (f32[256,256]{1,0:T(8,128)}, f32[1024,256]{1,0:T(8,128)}, f32[256,256]{0,1:T(8,128)})) %all-reduce.5.cloned.1.call-update) | async-done | bytes 1572880 | tf_op jit(solution)/shard_map/psum | solution.py:60
  620.6 1.6 select_reduce_fusion.2
  622.2 1.9 select_subtract_fusion.15
  624.1 2.0 fusion.8
  629.9 0.4 select_subtract_fusion.11
  634.1 1.8 fusion.36
  636.7 0.4 fusion.1
  637.5 1.0 select_reduce_fusion.1
  639.1 0.6 select_reduce_fusion
  639.8 1.2 select_subtract_fusion.7
  641.0 1.0 fusion.9
  647.7 0.8 fusion.34
  648.6 0.4 select_subtract_fusion.2
  651.7 0.8 convolution_bitcast_fusion.1
  652.9 73.3 %all-gather.5.cloned.1.call-done = f32[1024,256]{1,0:T(8,128)} async-done(((f32[16,256]{1,0:T(8,128)}), f32[1024,256]{1,0:T(8,128)}) %all-gather.5.cloned.1.call-update) | async-done | bytes 1048592 | tf_op jit(solution)/shard_map/all_gather | solution.py:68
  726.3 2.2 fusion.50
  728.7 2.9 fusion.3
  (69 shorter events, 17.4 us)
Async XLA Ops:
  7.2 37.6 %copy-start = (bf16[512,1024]{1,0:T(8,128)(2,1)S(1)}, bf16[512,1024]{1,0:T(8,128)(2,1)}, u32[]{:S(2)}) copy-start(bf16[512,1024]{1,0:T(8,128)(2,1)} %param.4) | copy-start | bytes 3145732
  7.2 37.6 %all-gather.3.cloned.1.call-start = ((), (), s32[]{:S(2)}) async-start(), calls=%async_computation.2 | async-start | bytes 1179648 | tf_op jit(solution)/shard_map/all_gather | solution.py:46
  7.9 41.3 %copy-start.4 = (f32[1,16,256]{2,1,0:T(8,128)S(1)}, f32[1,16,256]{2,1,0:T(8,128)}, u32[]{:S(2)}) copy-start(f32[1,16,256]{2,1,0:T(8,128)} %param.5) | copy-start | bytes 49156
  7.9 284.5 %reduce-scatter.2.cloned.1.call-start = ((), (), s32[]{:S(2)}) async-start(), calls=%async_computation.3 | async-start | bytes 4259840 | tf_op jit(solution)/shard_map/reduce_scatter | solution.py:48
  49.2 404.9 %all-reduce.7.cloned.1.call-start = ((), (), s32[]{:S(2)}) async-start(), calls=%async_computation.6 | async-start | bytes 2621440 | tf_op jit(solution)/shard_map/psum | solution.py:56
  292.4 166.9 %copy-start.2 = (f32[16,1024]{1,0:T(8,128)S(1)}, f32[16,1024]{1,0:T(8,128)}, u32[]{:S(2)}) copy-start(f32[16,1024]{1,0:T(8,128)} %reduce-scatter.2.cloned.1.call-done) | copy-start | bytes 196612
  295.4 325.2 %all-reduce.5.cloned.1.call-start = ((), (), s32[]{:S(2)}) async-start(), calls=%async_computation.5 | async-start | bytes 3145728 | tf_op jit(solution)/shard_map/psum | solution.py:60
  461.5 264.8 %all-gather.5.cloned.1.call-start = ((), (), s32[]{:S(2)}) async-start(), calls=%async_computation.4 | async-start | bytes 1064960 | tf_op jit(solution)/shard_map/all_gather | solution.py:68
  629.1 5.0 copy-start.1
  631.4 5.3 copy-start.3
  648.5 3.2 copy-start.5
Sparse Core Ops, SparseCore 0:
  10.1 34.5 all-gather.2
  49.3 243.0 reduce-scatter.1
  296.2 157.8 all-reduce.6
  461.6 158.9 all-reduce.4
  648.7 77.5 all-gather.4
where the time goes:
time: 742 us; the launch traced here: 738 us
  waiting for transfers between devices  650 us (88%)
  matrix products  48.7 us (7%)
  blocking collectives  18.5 us (2%)
  between operations  16.4 us (2%)
    reduce_scatter x1, waiting for transfers between devices, per_device(): lax.psum_scatter(lax.dot_general(whole, out_grads, (((0,), (0,)), ((), ()...  242 us
    psum x1, waiting for transfers between devices, per_device(): lax.psum((inner_rows(local_sketch, local_sketch), inner_rows(grad_part, l...  159 us
    psum x1, waiting for transfers between devices, per_device(): lax.psum((inner_rows(power, power), inner_rows(local_sketch, power), inne...  138 us
    all_gather x1, waiting for transfers between devices, per_device(): basis_full = lax.all_gather(basis_part, 'dp', axis=0, tiled=True)  73.3 us
    all_gather x1, waiting for transfers between devices, per_device(): whole = lax.all_gather(inputs, 'mp', axis=1, tiled=True)  36.8 us
    dot_general x57, matrix products, matmul(): jnp.dot(left, right, precision=lax.Precision.HIGHEST, preferred_element_t...  33.7 us
    all_to_all x1, blocking collectives, per_device(): lax.all_to_all(grad_part, 'dp', split_axis=1, concat_axis=0, tiled=True)  18.5 us
  transfers between devices with their start and end apart: 5, of which 5 were waited for; matrix products, arithmetic and copies ran while one was open for 1% of the time, Pallas kernels for 0%

commit v1 on v0

v1 whole, which is shorter than its diff:
```python
import jax
import jax.numpy as jnp
from jax import lax
from jax.experimental import pallas as pl
from jax.experimental.pallas import tpu as pltpu
from jax.sharding import Mesh, PartitionSpec as P

NS_ITERS = 8
BLOCK = 1024
RANK = 256
SIZES = (8, 8, 4, 2)
AXES = ("z", "y", "x", "core")
WIDTH = 16

NN = (((1,), (0,)), ((), ()))
NT = (((1,), (1,)), ((), ()))

THREE = ((0, 1), (1, 0), (0, 0))
FOUR = ((1, 1), (0, 1), (1, 0), (0, 0))
SIX = ((1, 1), (2, 0), (0, 2), (0, 1), (1, 0), (0, 0))


def matmul(left, right):
    return jnp.dot(left, right, precision=lax.Precision.HIGHEST, preferred_element_type=jnp.float32)


def split(value, count):
    pieces = []
    for step in range(count):
        piece = value.astype(jnp.bfloat16)
        pieces.append(piece)
        if step < count - 1:
            value = value - piece.astype(jnp.float32)
    return pieces


def product(left, right, terms, dims=NN):
    total = None
    for i, j in terms:
        term = lax.dot_general(left[i], right[j], dims, preferred_element_type=jnp.float32)
        total = term if total is None else total + term
    return total


def identity():
    rows = lax.broadcasted_iota(jnp.int32, (RANK, RANK), 0)
    cols = lax.broadcasted_iota(jnp.int32, (RANK, RANK), 1)
    return jnp.where(rows == cols, 1.0, 0.0).astype(jnp.float32)


def trace(matrix, ident):
    return jnp.sum(matrix * ident, keepdims=True)


def inverse_root(matrix, ident):
    scale = trace(matrix, ident)
    tmat = matrix * (1.0 / scale)
    zmat = 1.5 * ident - 0.5 * tmat
    for step in range(1, NS_ITERS):
        tsp = split(tmat, 2)
        square = product(tsp, tsp, FOUR)
        cube = product(split(square, 2), tsp, FOUR)
        tmat = 2.25 * tmat - 1.5 * square + 0.25 * cube
        zmat = 1.5 * zmat - 0.5 * product(split(zmat, 2), split(tmat, 2), THREE)
    return zmat * lax.rsqrt(scale)


def full_product(left, right, dims=NN):
    return product(split(left, 3), split(right, 3), SIX, dims)


def finish_kernel(place_ref, grad_ref, skt_ref, base_ref, upd_ref, fresh_ref, high_ref, low_ref, pick_ref, rows_ref, all_ref):
    for part in range(4):
        band = pl.ds(part * 256, 256)
        high, low = split(grad_ref[band, :], 2)
        high_ref[band, :] = high
        low_ref[band, :] = low
    block = pl.ds(pl.multiple_of(place_ref[0] * 128, 128), 128)
    inner = pl.ds(pl.multiple_of(place_ref[1] * WIDTH, WIDTH), WIDTH)
    moved = pl.ds(pl.multiple_of(place_ref[2] * 128, 128), 128)
    pick_ref[...] = grad_ref[:, block].T
    grad = (high_ref[...], low_ref[...])
    skt = skt_ref[...]
    wt = product(split(skt, 2), grad, THREE)
    power = base_ref[...] + product(split(wt, 2), grad, THREE, NT)
    psp = split(power, 3)
    gpow = product(psp, grad, THREE)
    ident = identity()
    gram = product(psp, psp, SIX, NT)
    spow = product(psp, split(skt, 3), SIX, NT)
    ritz = 0.95 * full_product(spow, spow, NT) + full_product(gpow, gpow, NT)
    cinv = inverse_root(gram, ident)
    csp = split(cinv, 3)
    hmat = product(split(product(csp, split(ritz, 3), SIX), 3), csp, SIX)
    eps = trace(hmat, ident) * (0.1 / RANK)
    hdamp = hmat + eps * ident
    rinv = inverse_root(hdamp, ident)
    root = full_product(hdamp, rinv)
    middle = jnp.sqrt(eps) * rinv - ident
    basis = product(csp, psp, SIX)
    bsp = split(basis, 3)
    cols = pick_ref[inner, :]
    coef = product(split(cols, 3), bsp, SIX, NT)
    upd_ref[...] = cols + product(split(full_product(coef, middle, NT), 3), bsp, SIX)
    all_ref[...] = basis
    rows_ref[...] = all_ref[:, moved].T
    fresh_ref[...] = full_product(rows_ref[inner, :], root)


def finish(place, grad, skt, base):
    whole = pl.BlockSpec(memory_space=pltpu.VMEM)
    return pl.pallas_call(
        finish_kernel,
        out_shape=(
            jax.ShapeDtypeStruct((WIDTH, BLOCK), jnp.float32),
            jax.ShapeDtypeStruct((WIDTH, RANK), jnp.float32),
        ),
        in_specs=[pl.BlockSpec(memory_space=pltpu.SMEM), whole, whole, whole],
        out_specs=(whole, whole),
        scratch_shapes=[
            pltpu.VMEM((BLOCK, BLOCK), jnp.bfloat16),
            pltpu.VMEM((BLOCK, BLOCK), jnp.bfloat16),
            pltpu.VMEM((128, BLOCK), jnp.float32),
            pltpu.VMEM((128, RANK), jnp.float32),
            pltpu.VMEM((RANK, BLOCK), jnp.float32),
        ],
        compiler_params=pltpu.CompilerParams(vmem_limit_bytes=40 * 1024 * 1024),
    )(place, grad, skt, base)


def groups(first):
    sets = []
    for x in range(SIZES[2]):
        for other in range(8):
            for core in range(2):
                along_y = (core == 0) == first
                sets.append([
                    (((other * 8 + i) if along_y else (i * 8 + other)) * SIZES[2] + x) * 2 + core
                    for i in range(8)
                ])
    return sets


def exchange(parts, axes, sets=None):
    return lax.all_to_all(
        parts, axes, split_axis=0, concat_axis=0, tiled=True, axis_index_groups=sets
    )


def gather(block, axes, size, sets=None):
    return exchange(jnp.broadcast_to(block[None], (size,) + block.shape), axes, sets)


def per_device(inputs, out_grads, sketch):
    near = gather(inputs, "x", SIZES[2])
    far = lax.ppermute(near, "core", [(0, 1), (1, 0)])
    core = lax.axis_index("core")
    part = lax.dot_general(
        jnp.concatenate([near, far]),
        out_grads,
        (((1,), (0,)), ((), ())),
        preferred_element_type=jnp.float32,
    ).reshape(BLOCK, BLOCK)
    one, two = groups(True), groups(False)
    band = lax.psum_scatter(part, AXES, scatter_dimension=0, tiled=True, axis_index_groups=one)
    own_sk = gather(sketch[0], "y", 8).reshape(-1, RANK)
    own_sk, band = lax.optimization_barrier((own_sk, band))
    rows = jnp.sum(exchange(band.reshape(8, WIDTH, BLOCK), AXES, two), axis=0)
    slab = gather(rows, AXES, 8, two).reshape(8 * WIDTH, BLOCK)
    grad = lax.all_gather(slab, AXES, axis=0, tiled=True, axis_index_groups=one)
    sk = gather(own_sk, "z", 8).reshape(4, 2, 128, RANK).swapaxes(0, 1)
    sk = jnp.where(core == 0, sk, sk[::-1]).reshape(BLOCK, RANK)
    skt = sk.T
    base = 0.95 * matmul(matmul(skt, sk), skt)
    z, y = lax.axis_index("z"), lax.axis_index("y")
    places = jnp.stack([z, y, (z % 2 + core) % 2 * 4 + z // 2])
    update, fresh = finish(places.astype(jnp.int32), grad, skt, base)
    update = update.reshape(WIDTH, 2, 4, 128)
    update = jnp.where(core == 0, update, update[:, ::-1])
    return (update.transpose(2, 1, 3, 0).reshape(1, BLOCK, WIDTH), fresh[None])


def solution(mesh):
    fine = Mesh(mesh.devices.reshape(SIZES), AXES)
    dp, mp = AXES[:2], AXES[2:]
    in_specs = (P(dp, mp), P(dp, mp), P(mp, dp, None))
    out_specs = (P(mp, None, dp), P(mp, dp, None))
    return jax.shard_map(
        per_device, mesh=fine, in_specs=in_specs, out_specs=out_specs, check_vma=False
    )
```

time: 742 us -> 201 us (0.27)
  waiting for transfers between devices: 650 us -> 76.4 us
  matrix products: 48.7 us -> 6.13 us
  blocking collectives: 18.5 us -> 56.9 us
  Pallas kernels: 0 us -> 25.4 us
  starting transfers between devices: 0.2 us -> 12.8 us
    psum x2 -> x0, waiting for transfers between devices: 297 us -> none  [the longest x1 159 us: per_device(): lax.psum((inner_rows(local_sketch, local_sketch), inner_rows(grad_part, l...]
    reduce_scatter x1, waiting for transfers between devices: 242 us -> 32 us  [per_device(): lax.psum_scatter(part, AXES, scatter_dimension=0, tiled=True, axis_index_...]
    all_gather x2 -> x1, waiting for transfers between devices: 110 us -> 15.2 us  [per_device(): grad = lax.all_gather(slab, AXES, axis=0, tiled=True, axis_index_groups=one)]
    all_to_all x1 -> x4, blocking collectives: 18.5 us -> 56.9 us  [exchange(): lax.all_to_all(parts, axes, split_axis=0, concat_axis=0, tiled=True, axis...]
    dot_general x57 -> x2, matrix products: 33.7 us -> 2.93 us  [matmul(): jnp.dot(left, right, precision=lax.Precision.HIGHEST, preferred_element_t...]
    all_to_all x0 -> x1, waiting for transfers between devices: none -> 27.7 us  [exchange(): lax.all_to_all(parts, axes, split_axis=0, concat_axis=0, tiled=True, axis...]
    pallas_call x0 -> x1, Pallas kernels: none -> 25.4 us  [finish(): pl.pallas_call(finish_kernel, out_shape=(jax.ShapeDtypeStruct((WIDTH, BLO...]
    dot_general x7 -> x1, matrix products: 15 us -> 3.2 us  [per_device(): lax.dot_general(jnp.concatenate([near, far]), out_grads, (((1,), (0,)), (...]
  transfers between devices with their start and end apart: 5 -> 4, of which waited for: 5 -> 4; matrix products, arithmetic and copies ran while one was open for 1% -> 4% of each run, Pallas kernels for 0% -> 0%
where the time goes in v1:
time: 201 us; the launch traced here: 200 us
  waiting for transfers between devices  76.4 us (38%)
  blocking collectives  56.9 us (28%)
  Pallas kernels  25.4 us (13%)
  between operations  14.1 us (7%)
  starting transfers between devices  12.8 us (6%)
  local copies, waits for them, and re-layouts  8.14 us (4%)
  matrix products  6.13 us (3%)
    all_to_all x4, blocking collectives, exchange(): lax.all_to_all(parts, axes, split_axis=0, concat_axis=0, tiled=True, axis...  56.9 us
    reduce_scatter x1, waiting for transfers between devices, per_device(): lax.psum_scatter(part, AXES, scatter_dimension=0, tiled=True, axis_index_...  32 us
    all_to_all x1, waiting for transfers between devices, exchange(): lax.all_to_all(parts, axes, split_axis=0, concat_axis=0, tiled=True, axis...  27.7 us
    pallas_call x1, Pallas kernels, finish(): pl.pallas_call(finish_kernel, out_shape=(jax.ShapeDtypeStruct((WIDTH, BLO...  25.4 us
    all_gather x1, waiting for transfers between devices, per_device(): grad = lax.all_gather(slab, AXES, axis=0, tiled=True, axis_index_groups=one)  15.2 us
    ppermute x1, starting transfers between devices, per_device(): far = lax.ppermute(near, 'core', [(0, 1), (1, 0)])  7.81 us
    all_to_all x1, starting transfers between devices, exchange(): lax.all_to_all(parts, axes, split_axis=0, concat_axis=0, tiled=True, axis...  4.89 us
  transfers between devices with their start and end apart: 4, of which 4 were waited for; matrix products, arithmetic and copies ran while one was open for 4% of the time, Pallas kernels for 0%

profile of v1, /device:TPU:1, one launch (start us, length us, event | category | flops | bytes accessed | tf_op | source)
XLA Modules:
  0.0 200.1 jit_solution(16633397058021257231)
XLA Ops:
  7.2 0.0 copy-start
  7.2 0.0 reduce-scatter.2.cloned.1.call-start
  7.2 1.1 copy.7
  8.4 11.6 %all_to_all.25 = bf16[4,512,128]{1,2,0:T(8,128)(2,1)S(1)} all-to-all(bf16[4,512,128]{1,2,0:T(8,128)(2,1)S(1)} %broadcast_in_dim.14), channel_id=1, replica_groups=mesh['z'=8,'y'=8,'x'=4,'core'=2] {'x'}, dimensions={0} | all-to-all | bytes 1048576 | tf_op jit(solution)/shard_map/all_to_all | solution.py:145
  19.9 0.0 copy-start.2
  19.9 7.8 %collective-permute-start = (bf16[4,512,128]{1,2,0:T(8,128)(2,1)S(1)}, bf16[4,512,128]{1,2,0:T(8,128)(2,1)S(1)}, u32[]{:S(2)}, u32[]{:S(2)}) collective-permute-start(bf16[4,512,128]{1,2,0:T(8,128)(2,1)S(1)} %all_to_all.25), channel_id=1, source_target_pairs={{0,1},{1,0},{2,3},{3,2},{4,5},{5,4},{6,7},{7,6},{8,9},{9,8},{10,11... | collective-permute-start | bytes 1572872 | tf_op jit(solution)/shard_map/ppermute | solution.py:156
  27.8 1.5 collective-permute-done
  29.3 0.0 copy-done
  29.3 3.2 %fusion = f32[8,128,1024]{2,1,0:T(8,128)} fusion(bf16[4,512,128]{1,2,0:T(8,128)(2,1)S(1)} %collective-permute-done, bf16[4,512,128]{1,2,0:T(8,128)(2,1)S(1)} %all_to_all.25, bf16[512,1024]{1,0:T(8,128)(2,1)S(1)} %copy-done), kind=kOutput, calls=%fused_computation.3 | convolution fusion | flops 1074266112 | bytes 6291456 | tf_op jit(solution)/shard_map/dot_general | solution.py:158
  32.5 0.0 reduce-scatter.2.cloned.1.call-update
  32.5 0.0 all-gather.2.cloned.1.call-start
  32.6 0.0 copy-done.2
  32.6 12.2 %all_to_all.26 = f32[8,16,256]{2,1,0:T(8,128)S(1)} all-to-all(f32[8,16,256]{2,1,0:T(8,128)S(1)} %broadcast_in_dim.13), channel_id=1, replica_groups=mesh['z'=8,'y'=8,'x'=4,'core'=2] {'y'}, dimensions={0} | all-to-all | bytes 262144 | tf_op jit(solution)/shard_map/all_to_all | solution.py:145
  44.8 32.0 %reduce-scatter.2.cloned.1.call-done = f32[128,1024]{1,0:T(8,128)} async-done(((f32[1024,1024]{1,0:T(8,128)}), f32[128,1024]{1,0:T(8,128)}) %reduce-scatter.2.cloned.1.call-update) | async-done | bytes 524304 | tf_op jit(solution)/shard_map/reduce_scatter | solution.py:165
  76.8 17.9 %all_to_all.27 = f32[8,16,1024]{2,1,0:T(8,128)S(1)} all-to-all(f32[8,16,1024]{2,1,0:T(8,128)} %bitcast.33), channel_id=1, replica_groups={{0,64,128,192,256,320,384,448},{1,9,17,25,33,41,49,57},{8,72,136,200,26..., dimensions={0} | all-to-all | bytes 1048576 | tf_op jit(solution)/shard_map/all_to_all | solution.py:145
  94.8 15.2 %all_to_all.28 = f32[8,16,1024]{2,1,0:T(8,128)} all-to-all(f32[8,16,1024]{2,1,0:T(8,128)S(1)} %broadcast_in_dim.15), channel_id=1, replica_groups={{0,64,128,192,256,320,384,448},{1,9,17,25,33,41,49,57},{8,72,136,200,26..., dimensions={0} | all-to-all | bytes 1048576 | tf_op jit(solution)/shard_map/all_to_all | solution.py:145
  110.0 0.0 all-gather.2.cloned.1.call-update
  110.0 1.1 broadcast_in_dim.32
  111.1 4.9 %all-to-all-start.4 = ((f32[8,128,256]{2,1,0:T(8,128)}), f32[8,128,256]{2,1,0:T(8,128)S(1)}, u32[]{:S(2)}, u32[]{:S(2)}) async-start(f32[8,128,256]{2,1,0:T(8,128)} %broadcast_in_dim.32), calls=%async_computation.5 | async-start | bytes 2097152 | tf_op jit(solution)/shard_map/all_to_all | solution.py:145
  116.0 0.1 pad_add_fusion.place_ref
  116.1 27.7 %all-to-all-done.4 = f32[8,128,256]{2,1,0:T(8,128)S(1)} async-done(((f32[8,128,256]{2,1,0:T(8,128)}), f32[8,128,256]{2,1,0:T(8,128)S(1)}, u32[]{:S(2)}, u32[]{:S(2)}) %all-to-all-start.4) | async-done | bytes 1048608 | tf_op jit(solution)/shard_map/all_to_all | solution.py:145
  143.8 0.1 reverse_select_fusion
  143.9 1.3 copy.8
  145.2 1.6 reshape.36
  146.8 1.9 convolution_bitcast_fusion
  148.7 1.0 convolution_multiply_fusion.base_ref
  149.8 15.2 %all-gather.2.cloned.1.call-done.grad_ref = f32[1024,1024]{1,0:T(8,128)} async-done(((f32[128,1024]{1,0:T(8,128)}), f32[1024,1024]{1,0:T(8,128)}) %all-gather.2.cloned.1.call-update) | async-done | bytes 4194320 | tf_op jit(solution)/shard_map/all_gather | solution.py:170
  164.9 0.0 copy-start.1
  164.9 2.2 %copy-done.1 = f32[1024,1024]{1,0:T(8,128)S(1)} copy-done((f32[1024,1024]{1,0:T(8,128)S(1)}, f32[1024,1024]{1,0:T(8,128)}, u32[]{:S(2)}) %copy-start.1) | copy-done | bytes 4194328
  167.1 25.4 %shard_map.50 = (f32[16,1024]{1,0:T(8,128)S(1)}, f32[16,256]{1,0:T(8,128)}) custom-call(s32[3]{0:T(128)S(1)} %pad_add_fusion.place_ref, f32[1024,1024]{1,0:T(8,128)S(1)} %copy-done.1, f32[256,1024]{1,0:T(8,128)S(1)} %bitcast.28, f32[256,1024]{1,0:T(8,128)S(1)} %convolution_multiply_fusion.base_ref), custom_call_target="tpu_custom_call" | custom-call | tf_op jit(solution)/shard_map/pallas_call | solution.py:112
  192.6 0.7 reshape.38
  (7 shorter events, 0.2 us)
Async XLA Ops:
  7.2 22.1 %copy-start = (bf16[512,1024]{1,0:T(8,128)(2,1)S(1)}, bf16[512,1024]{1,0:T(8,128)(2,1)}, u32[]{:S(2)}) copy-start(bf16[512,1024]{1,0:T(8,128)(2,1)} %param.4) | copy-start | bytes 3145732
  7.2 69.6 %reduce-scatter.2.cloned.1.call-start = ((), (), s32[]{:S(2)}) async-start(), calls=%async_computation.6 | async-start | bytes 4718592 | tf_op jit(solution)/shard_map/reduce_scatter | solution.py:165
  19.9 12.6 %copy-start.2 = (f32[1,16,256]{2,1,0:T(8,128)S(1)}, f32[1,16,256]{2,1,0:T(8,128)}, u32[]{:S(2)}) copy-start(f32[1,16,256]{2,1,0:T(8,128)} %param.5) | copy-start | bytes 49156
  19.9 9.3 %collective-permute-start = (bf16[4,512,128]{1,2,0:T(8,128)(2,1)S(1)}, bf16[4,512,128]{1,2,0:T(8,128)(2,1)S(1)}, u32[]{:S(2)}, u32[]{:S(2)}) collective-permute-start(bf16[4,512,128]{1,2,0:T(8,128)(2,1)S(1)} %all_to_all.25), channel_id=1, source_target_pairs={{0,1},{1,0},{2,3},{3,2},{4,5},{5,4},{6,7},{7,6},{8,9},{9,8},{10,11... | collective-permute-start | bytes 1572872 | tf_op jit(solution)/shard_map/ppermute | solution.py:156
  32.5 132.4 %all-gather.2.cloned.1.call-start = ((), (), s32[]{:S(2)}) async-start(), calls=%async_computation.7 | async-start | bytes 4718592 | tf_op jit(solution)/shard_map/all_gather | solution.py:170
  111.1 32.7 %all-to-all-start.4 = ((f32[8,128,256]{2,1,0:T(8,128)}), f32[8,128,256]{2,1,0:T(8,128)S(1)}, u32[]{:S(2)}, u32[]{:S(2)}) async-start(f32[8,128,256]{2,1,0:T(8,128)} %broadcast_in_dim.32), calls=%async_computation.5 | async-start | bytes 2097152 | tf_op jit(solution)/shard_map/all_to_all | solution.py:145
  164.9 2.2 %copy-start.1 = (f32[1024,1024]{1,0:T(8,128)S(1)}, f32[1024,1024]{1,0:T(8,128)}, u32[]{:S(2)}) copy-start(f32[1024,1024]{1,0:T(8,128)} %all-gather.2.cloned.1.call-done.grad_ref) | copy-start | bytes 12582916
Sparse Core Ops, SparseCore 0:
  32.6 44.1 reduce-scatter.1
  110.2 54.7 all-gather.1

commit v2 on v1

v2 whole, which is shorter than its diff:
```python
import jax
import jax.numpy as jnp
from jax import lax
from jax.experimental import pallas as pl
from jax.experimental.pallas import tpu as pltpu
from jax.sharding import Mesh, PartitionSpec as P

NS_ITERS = 8
BLOCK = 1024
RANK = 256
SIZES = (8, 8, 4, 2)
AXES = ("z", "y", "x", "core")
WIDTH = 16
PARTS = 4
BAND = BLOCK // PARTS

NN = (((1,), (0,)), ((), ()))
NT = (((1,), (1,)), ((), ()))

THREE = ((0, 1), (1, 0), (0, 0))
SIX = ((1, 1), (2, 0), (0, 2), (0, 1), (1, 0), (0, 0))


def split(value, count):
    pieces = []
    for step in range(count):
        piece = value.astype(jnp.bfloat16)
        pieces.append(piece)
        if step < count - 1:
            value = value - piece.astype(jnp.float32)
    return pieces


def product(left, right, terms, dims=NN):
    total = None
    for i, j in terms:
        term = lax.dot_general(left[i], right[j], dims, preferred_element_type=jnp.float32)
        total = term if total is None else total + term
    return total


def identity():
    rows = lax.broadcasted_iota(jnp.int32, (RANK, RANK), 0)
    cols = lax.broadcasted_iota(jnp.int32, (RANK, RANK), 1)
    return jnp.where(rows == cols, 1.0, 0.0).astype(jnp.float32)


def trace(matrix, ident):
    return jnp.sum(matrix * ident, keepdims=True)


def own_product(value):
    one, two, three = split(value, 3)
    cross = lax.dot_general(
        jnp.concatenate([one, one], axis=1),
        jnp.concatenate([three, two], axis=1),
        NT,
        preferred_element_type=jnp.float32,
    )
    return (cross + cross.T) + product((one, two), (one, two), ((1, 1), (0, 0)), NT)


def inverse_root(matrix, ident):
    scale = trace(matrix, ident)
    tmat = matrix * (1.0 / scale)
    zmat = 1.5 * ident - 0.5 * tmat
    for step in range(1, NS_ITERS):
        tsp = split(tmat, 2)
        square = product(tsp, tsp, THREE)
        cube = product(split(square, 2), tsp, THREE)
        tmat = 2.25 * tmat - 1.5 * square + 0.25 * cube
        zmat = 1.5 * zmat - 0.5 * product(split(zmat, 2), split(tmat, 2), THREE)
    return zmat * lax.rsqrt(scale)


def full_product(left, right):
    return product(split(left, 3), split(right, 3), SIX)


def finish_kernel(
    place_ref, both_ref, upd_ref, fresh_ref,
    wide_ref, high_ref, low_ref, all_ref, pow_ref, pick_ref, rows_ref, sems,
):
    copies = []
    for part in range(PARTS):
        band = pl.ds(part * BAND, BAND)
        copies.append(pltpu.make_async_copy(both_ref.at[band, :], wide_ref.at[band, :], sems.at[part]))
        copies[-1].start()
    wt = None
    for part in range(PARTS):
        copies[part].wait()
        band = pl.ds(part * BAND, BAND)
        high, low = split(wide_ref[band, :], 2)
        high_ref[band, :] = high
        low_ref[band, :] = low
        skt = wide_ref[band, BLOCK:].T
        term = product(split(skt, 2), (high, low), THREE)
        wt = term if wt is None else wt + term
    block = pl.ds(pl.multiple_of(place_ref[0] * 128, 128), 128)
    inner = pl.ds(pl.multiple_of(place_ref[1] * WIDTH, WIDTH), WIDTH)
    moved = pl.ds(pl.multiple_of(place_ref[2] * 128, 128), 128)
    lane = lax.broadcasted_iota(jnp.int32, (1, BLOCK + RANK), 1)

    both = (high_ref[...], low_ref[...])
    power = product(split(wt * jnp.where(lane < BLOCK, 1.0, 0.95), 2), both, THREE, NT)
    ident = identity()
    psp = split(power, 3)
    gram = own_product(power)
    gpow = product(psp, both, THREE)
    ritz = own_product(gpow * jnp.where(lane < BLOCK, 1.0, 0.95 ** 0.5))
    cinv = inverse_root(gram, ident)
    csp = split(cinv, 3)
    pick_ref[...] = wide_ref[:, block].T
    cols = pick_ref[inner, :]
    pow_ref[...] = power
    rows_ref[...] = pow_ref[:, moved].T
    prow = rows_ref[inner, :]
    all_ref[...] = gpow
    rows_ref[...] = all_ref[:, block].T
    gcol = rows_ref[inner, :]
    pair = product(split(jnp.concatenate([prow, gcol], axis=0), 3), csp, SIX)
    hmat = product(split(product(csp, split(ritz, 3), SIX), 3), csp, SIX)
    eps = trace(hmat, ident) * (0.1 / RANK)
    hdamp = hmat + eps * ident
    lead = full_product(pair[:WIDTH], hdamp)
    rinv = inverse_root(hdamp, ident)
    last = full_product(jnp.concatenate([lead, pair[WIDTH:]], axis=0), rinv)
    fresh_ref[...] = last[:WIDTH]
    middle = jnp.sqrt(eps) * last[WIDTH:] - pair[WIDTH:]
    coef = product(split(middle, 3), csp, SIX)
    upd_ref[...] = cols + product(split(coef, 3), psp, SIX)


def finish(places, both):
    whole = pl.BlockSpec(memory_space=pltpu.VMEM)
    return pl.pallas_call(
        finish_kernel,
        out_shape=(
            jax.ShapeDtypeStruct((WIDTH, BLOCK), jnp.float32),
            jax.ShapeDtypeStruct((WIDTH, RANK), jnp.float32),
        ),
        in_specs=[pl.BlockSpec(memory_space=pltpu.SMEM), pl.BlockSpec(memory_space=pltpu.HBM)],
        out_specs=(whole, whole),
        scratch_shapes=[
            pltpu.VMEM((BLOCK, BLOCK + RANK), jnp.float32),
            pltpu.VMEM((BLOCK, BLOCK + RANK), jnp.bfloat16),
            pltpu.VMEM((BLOCK, BLOCK + RANK), jnp.bfloat16),
            pltpu.VMEM((RANK, BLOCK + RANK), jnp.float32),
            pltpu.VMEM((RANK, BLOCK), jnp.float32),
            pltpu.VMEM((128, BLOCK), jnp.float32),
            pltpu.VMEM((128, RANK), jnp.float32),
            pltpu.SemaphoreType.DMA((PARTS,)),
        ],
        compiler_params=pltpu.CompilerParams(vmem_limit_bytes=48 * 1024 * 1024),
    )(places, both)


def groups(first):
    sets = []
    for x in range(SIZES[2]):
        for other in range(8):
            for core in range(2):
                along_y = (core == 0) == first
                sets.append([
                    (((other * 8 + i) if along_y else (i * 8 + other)) * SIZES[2] + x) * 2 + core
                    for i in range(8)
                ])
    return sets


def sketch_moves():
    nz, ny, nx, nc = SIZES
    moves = []
    for z in range(nz):
        for y in range(ny):
            for x in range(nx):
                for core in range(nc):
                    position, inner = (y, z) if core == 0 else (z, y)
                    natural = position % 4 * 2 + (position // 4 + core) % 2
                    source = ((natural * ny + inner) * nx + x) * nc + core
                    moves.append((source, ((z * ny + y) * nx + x) * nc + core))
    return moves


def exchange(parts, axes, sets=None):
    return lax.all_to_all(
        parts, axes, split_axis=0, concat_axis=0, tiled=True, axis_index_groups=sets
    )


def gather(block, axes, size, sets=None):
    return exchange(jnp.broadcast_to(block[None], (size,) + block.shape), axes, sets)


def per_device(inputs, out_grads, sketch):
    near = gather(inputs, "x", SIZES[2])
    far = lax.ppermute(near, "core", [(0, 1), (1, 0)])
    core = lax.axis_index("core")
    part = lax.dot_general(
        jnp.concatenate([near, far]),
        out_grads,
        (((1,), (0,)), ((), ())),
        preferred_element_type=jnp.float32,
    ).reshape(BLOCK, BLOCK)
    part, own_sk = lax.optimization_barrier((part, sketch[0]))
    one, two = groups(True), groups(False)
    band = lax.psum_scatter(part, AXES, scatter_dimension=0, tiled=True, axis_index_groups=one)
    own_sk = lax.ppermute(own_sk, AXES, sketch_moves())
    rows = jnp.sum(exchange(band.reshape(8, WIDTH, BLOCK), AXES, two), axis=0)
    rows = jnp.concatenate([rows, own_sk], axis=1)
    slab = gather(rows, AXES, 8, two).reshape(8 * WIDTH, BLOCK + RANK)
    both = lax.all_gather(slab, AXES, axis=0, tiled=True, axis_index_groups=one)
    z, y = lax.axis_index("z"), lax.axis_index("y")
    places = jnp.stack([z, y, (z % 2 + core) % 2 * 4 + z // 2])
    update, fresh = finish(places.astype(jnp.int32), both)
    update = update.reshape(WIDTH, 2, 4, 128)
    update = jnp.where(core == 0, update, update[:, ::-1])
    return (update.transpose(2, 1, 3, 0).reshape(1, BLOCK, WIDTH), fresh[None])


def solution(mesh):
    fine = Mesh(mesh.devices.reshape(SIZES), AXES)
    dp, mp = AXES[:2], AXES[2:]
    in_specs = (P(dp, mp), P(dp, mp), P(mp, dp, None))
    out_specs = (P(mp, None, dp), P(mp, dp, None))
    return jax.shard_map(
        per_device, mesh=fine, in_specs=in_specs, out_specs=out_specs, check_vma=False
    )
```

time: 201 us -> 192 us (0.955)
  blocking collectives: 56.9 us -> 28.2 us
  waiting for transfers between devices: 76.4 us -> 98.5 us
  starting transfers between devices: 12.8 us -> 18.9 us
  local copies, waits for them, and re-layouts: 8.14 us -> 4.42 us
  matrix products: 6.13 us -> 3.19 us
  Pallas kernels: 25.4 us -> 23 us
    all_gather x1, waiting for transfers between devices: 15.2 us -> 46 us  [per_device(): both = lax.all_gather(slab, AXES, axis=0, tiled=True, axis_index_groups=one)]
    all_to_all x4 -> x2, blocking collectives: 56.9 us -> 28.2 us  [exchange(): lax.all_to_all(parts, axes, split_axis=0, concat_axis=0, tiled=True, axis...]
    all_to_all x1, waiting for transfers between devices: 27.7 us -> 6.82 us  [exchange(): lax.all_to_all(parts, axes, split_axis=0, concat_axis=0, tiled=True, axis...]
    reduce_scatter x1, waiting for transfers between devices: 32 us -> 44.2 us  [per_device(): lax.psum_scatter(part, AXES, scatter_dimension=0, tiled=True, axis_index_...]
    ppermute x0 -> x1, starting transfers between devices: none -> 5.26 us  [per_device(): own_sk = lax.ppermute(own_sk, AXES, sketch_moves())]
    dot_general x2 -> x0, matrix products: 2.93 us -> none  [matmul(): jnp.dot(left, right, precision=lax.Precision.HIGHEST, preferred_element_t...]
    pallas_call x1, Pallas kernels: 25.4 us -> 23 us  [finish(): pl.pallas_call(finish_kernel, out_shape=(jax.ShapeDtypeStruct((WIDTH, BLO...]
  transfers between devices with their start and end apart: 4 -> 5, of which waited for: 4 -> 4; matrix products, arithmetic and copies ran while one was open for 4% -> 0% of each run, Pallas kernels for 0% -> 0%
where the time goes in v2:
time: 192 us; the launch traced here: 191 us
  waiting for transfers between devices  98.5 us (51%)
  blocking collectives  28.2 us (15%)
  Pallas kernels  23 us (12%)
  starting transfers between devices  18.9 us (10%)
  between operations  14.2 us (7%)
  local copies, waits for them, and re-layouts  4.42 us (2%)
  matrix products  3.19 us (2%)
    all_gather x1, waiting for transfers between devices, per_device(): both = lax.all_gather(slab, AXES, axis=0, tiled=True, axis_index_groups=one)  46 us
    reduce_scatter x1, waiting for transfers between devices, per_device(): lax.psum_scatter(part, AXES, scatter_dimension=0, tiled=True, axis_index_...  44.2 us
    all_to_all x2, blocking collectives, exchange(): lax.all_to_all(parts, axes, split_axis=0, concat_axis=0, tiled=True, axis...  28.2 us
    pallas_call x1, Pallas kernels, finish(): pl.pallas_call(finish_kernel, out_shape=(jax.ShapeDtypeStruct((WIDTH, BLO...  23 us
    ppermute x1, starting transfers between devices, per_device(): far = lax.ppermute(near, 'core', [(0, 1), (1, 0)])  7.68 us
    all_to_all x1, waiting for transfers between devices, exchange(): lax.all_to_all(parts, axes, split_axis=0, concat_axis=0, tiled=True, axis...  6.82 us
    all_to_all x1, starting transfers between devices, exchange(): lax.all_to_all(parts, axes, split_axis=0, concat_axis=0, tiled=True, axis...  5.88 us
    ppermute x1, starting transfers between devices, per_device(): own_sk = lax.ppermute(own_sk, AXES, sketch_moves())  5.26 us
  transfers between devices with their start and end apart: 5, of which 4 were waited for; matrix products, arithmetic and copies ran while one was open for 0% of the time, Pallas kernels for 0%

profile of v2, /device:TPU:1, one launch (start us, length us, event | category | flops | bytes accessed | tf_op | source)
XLA Modules:
  0.0 190.6 jit_solution(12546825273333619804)
XLA Ops:
  7.2 0.0 copy-start
  7.2 0.0 reduce-scatter.2.cloned.1.call-start
  7.2 1.1 copy.5
  8.4 11.6 %all_to_all.15 = bf16[4,512,128]{1,2,0:T(8,128)(2,1)S(1)} all-to-all(bf16[4,512,128]{1,2,0:T(8,128)(2,1)S(1)} %broadcast_in_dim.6), channel_id=1, replica_groups=mesh['z'=8,'y'=8,'x'=4,'core'=2] {'x'}, dimensions={0} | all-to-all | bytes 1048576 | tf_op jit(solution)/shard_map/all_to_all | solution.py:186
  19.9 7.7 %collective-permute-start = (bf16[4,512,128]{1,2,0:T(8,128)(2,1)S(1)}, bf16[4,512,128]{1,2,0:T(8,128)(2,1)S(1)}, u32[]{:S(2)}, u32[]{:S(2)}) collective-permute-start(bf16[4,512,128]{1,2,0:T(8,128)(2,1)S(1)} %all_to_all.15), channel_id=1, source_target_pairs={{0,1},{1,0},{2,3},{3,2},{4,5},{5,4},{6,7},{7,6},{8,9},{9,8},{10,11... | collective-permute-start | bytes 1572872 | tf_op jit(solution)/shard_map/ppermute | solution.py:197
  27.6 1.5 collective-permute-done
  29.1 0.0 copy-done
  29.1 3.2 %fusion = f32[8,128,1024]{2,1,0:T(8,128)} fusion(bf16[4,512,128]{1,2,0:T(8,128)(2,1)S(1)} %collective-permute-done, bf16[4,512,128]{1,2,0:T(8,128)(2,1)S(1)} %all_to_all.15, bf16[512,1024]{1,0:T(8,128)(2,1)S(1)} %copy-done), kind=kOutput, calls=%fused_computation | convolution fusion | flops 1074266112 | bytes 6291456 | tf_op jit(solution)/shard_map/dot_general | solution.py:199
  32.3 0.0 copy-start.2
  32.3 0.0 reduce-scatter.2.cloned.1.call-update
  32.4 44.2 %reduce-scatter.2.cloned.1.call-done = f32[128,1024]{1,0:T(8,128)} async-done(((f32[1024,1024]{1,0:T(8,128)}), f32[128,1024]{1,0:T(8,128)}) %reduce-scatter.2.cloned.1.call-update) | async-done | bytes 524304 | tf_op jit(solution)/shard_map/reduce_scatter | solution.py:207
  76.5 5.9 %all-to-all-start.1 = ((f32[8,16,1024]{2,1,0:T(8,128)}), f32[8,16,1024]{2,1,0:T(8,128)S(1)}, u32[]{:S(2)}, u32[]{:S(2)}) async-start(f32[8,16,1024]{2,1,0:T(8,128)} %bitcast.17), calls=%async_computation.2 | async-start | bytes 1048576 | tf_op jit(solution)/shard_map/all_to_all | solution.py:186
  82.4 0.0 all-gather.2.cloned.1.call-start
  82.5 0.0 copy-done.2
  82.5 5.3 %collective-permute-start.1 = (f32[16,256]{1,0:T(8,128)S(1)}, f32[16,256]{1,0:T(8,128)S(1)}, u32[]{:S(2)}, u32[]{:S(2)}) collective-permute-start(f32[16,256]{1,0:T(8,128)S(1)} %bitcast.18), channel_id=1, source_target_pairs={{0,0},{65,1},{2,2},{67,3},{4,4},{69,5},{6,6},{71,7},{128,8},{73,9}... | collective-permute-start | bytes 49160 | tf_op jit(solution)/shard_map/ppermute | solution.py:208
  87.7 6.8 %all-to-all-done.1 = f32[8,16,1024]{2,1,0:T(8,128)S(1)} async-done(((f32[8,16,1024]{2,1,0:T(8,128)}), f32[8,16,1024]{2,1,0:T(8,128)S(1)}, u32[]{:S(2)}, u32[]{:S(2)}) %all-to-all-start.1) | async-done | bytes 524320 | tf_op jit(solution)/shard_map/all_to_all | solution.py:186
  94.6 0.0 collective-permute-done.1
  94.7 16.6 %all_to_all.16 = f32[8,16,1280]{2,1,0:T(8,128)} all-to-all(f32[8,16,1280]{2,1,0:T(8,128)S(1)} %broadcast_in_dim.7), channel_id=1, replica_groups={{0,64,128,192,256,320,384,448},{1,9,17,25,33,41,49,57},{8,72,136,200,26..., dimensions={0} | all-to-all | bytes 1310720 | tf_op jit(solution)/shard_map/all_to_all | solution.py:186
  111.3 0.0 all-gather.2.cloned.1.call-update
  111.4 0.1 pad_add_fusion.place_ref
  111.5 46.0 %all-gather.2.cloned.1.call-done.both_ref = f32[1024,1280]{1,0:T(8,128)} async-done(((f32[128,1280]{1,0:T(8,128)}), f32[1024,1280]{1,0:T(8,128)}) %all-gather.2.cloned.1.call-update) | async-done | bytes 5242896 | tf_op jit(solution)/shard_map/all_gather | solution.py:212
  157.4 0.0 copy-start.1
  157.4 2.5 %copy-done.1 = f32[1024,1280]{1,0:T(8,128)S(1)} copy-done((f32[1024,1280]{1,0:T(8,128)S(1)}, f32[1024,1280]{1,0:T(8,128)}, u32[]{:S(2)}) %copy-start.1) | copy-done | bytes 5242904
  159.9 23.0 %shard_map.50 = (f32[16,1024]{1,0:T(8,128)S(1)}, f32[16,256]{1,0:T(8,128)}) custom-call(s32[3]{0:T(128)S(1)} %pad_add_fusion.place_ref, f32[1024,1280]{1,0:T(8,128)S(1)} %copy-done.1), custom_call_target="tpu_custom_call" | custom-call | tf_op jit(solution)/shard_map/pallas_call | solution.py:136
  183.1 0.7 reshape.25
  (7 shorter events, 0.2 us)
Async XLA Ops:
  7.2 22.0 %copy-start = (bf16[512,1024]{1,0:T(8,128)(2,1)S(1)}, bf16[512,1024]{1,0:T(8,128)(2,1)}, u32[]{:S(2)}) copy-start(bf16[512,1024]{1,0:T(8,128)(2,1)} %param.4) | copy-start | bytes 3145732
  7.2 69.4 %reduce-scatter.2.cloned.1.call-start = ((), (), s32[]{:S(2)}) async-start(), calls=%async_computation.4 | async-start | bytes 4718592 | tf_op jit(solution)/shard_map/reduce_scatter | solution.py:207
  19.9 9.2 %collective-permute-start = (bf16[4,512,128]{1,2,0:T(8,128)(2,1)S(1)}, bf16[4,512,128]{1,2,0:T(8,128)(2,1)S(1)}, u32[]{:S(2)}, u32[]{:S(2)}) collective-permute-start(bf16[4,512,128]{1,2,0:T(8,128)(2,1)S(1)} %all_to_all.15), channel_id=1, source_target_pairs={{0,1},{1,0},{2,3},{3,2},{4,5},{5,4},{6,7},{7,6},{8,9},{9,8},{10,11... | collective-permute-start | bytes 1572872 | tf_op jit(solution)/shard_map/ppermute | solution.py:197
  32.3 50.1 %copy-start.2 = (f32[1,16,256]{2,1,0:T(8,128)S(1)}, f32[1,16,256]{2,1,0:T(8,128)}, u32[]{:S(2)}) copy-start(f32[1,16,256]{2,1,0:T(8,128)} %param.5) | copy-start | bytes 49156
  76.5 18.0 %all-to-all-start.1 = ((f32[8,16,1024]{2,1,0:T(8,128)}), f32[8,16,1024]{2,1,0:T(8,128)S(1)}, u32[]{:S(2)}, u32[]{:S(2)}) async-start(f32[8,16,1024]{2,1,0:T(8,128)} %bitcast.17), calls=%async_computation.2 | async-start | bytes 1048576 | tf_op jit(solution)/shard_map/all_to_all | solution.py:186
  82.4 75.0 %all-gather.2.cloned.1.call-start = ((), (), s32[]{:S(2)}) async-start(), calls=%async_computation.5 | async-start | bytes 5898240 | tf_op jit(solution)/shard_map/all_gather | solution.py:212
  82.5 12.1 %collective-permute-start.1 = (f32[16,256]{1,0:T(8,128)S(1)}, f32[16,256]{1,0:T(8,128)S(1)}, u32[]{:S(2)}, u32[]{:S(2)}) collective-permute-start(f32[16,256]{1,0:T(8,128)S(1)} %bitcast.18), channel_id=1, source_target_pairs={{0,0},{65,1},{2,2},{67,3},{4,4},{69,5},{6,6},{71,7},{128,8},{73,9}... | collective-permute-start | bytes 49160 | tf_op jit(solution)/shard_map/ppermute | solution.py:208
  157.4 2.5 %copy-start.1 = (f32[1024,1280]{1,0:T(8,128)S(1)}, f32[1024,1280]{1,0:T(8,128)}, u32[]{:S(2)}) copy-start(f32[1024,1280]{1,0:T(8,128)} %all-gather.2.cloned.1.call-done.both_ref) | copy-start | bytes 15728644
Sparse Core Ops, SparseCore 0:
  32.5 44.0 reduce-scatter.1
  111.5 45.9 all-gather.1

commit v3 on v2

--- a/solution.py
+++ b/solution.py
@@ -11,7 +11,7 @@
 SIZES = (8, 8, 4, 2)
 AXES = ("z", "y", "x", "core")
 WIDTH = 16
-PARTS = 4
+PARTS = 2
 BAND = BLOCK // PARTS
 
 NN = (((1,), (0,)), ((), ()))
@@ -60,13 +60,14 @@
     return (cross + cross.T) + product((one, two), (one, two), ((1, 1), (0, 0)), NT)
 
 
-def inverse_root(matrix, ident):
+def inverse_root(matrix, ident, beside=lambda step: None):
     scale = trace(matrix, ident)
     tmat = matrix * (1.0 / scale)
     zmat = 1.5 * ident - 0.5 * tmat
     for step in range(1, NS_ITERS):
         tsp = split(tmat, 2)
         square = product(tsp, tsp, THREE)
+        beside(step)
         cube = product(split(square, 2), tsp, THREE)
         tmat = 2.25 * tmat - 1.5 * square + 0.25 * cube
         zmat = 1.5 * zmat - 0.5 * product(split(zmat, 2), split(tmat, 2), THREE)
@@ -99,23 +100,31 @@
     block = pl.ds(pl.multiple_of(place_ref[0] * 128, 128), 128)
     inner = pl.ds(pl.multiple_of(place_ref[1] * WIDTH, WIDTH), WIDTH)
     moved = pl.ds(pl.multiple_of(place_ref[2] * 128, 128), 128)
+
+    both = (high_ref[...], low_ref[...])
     lane = lax.broadcasted_iota(jnp.int32, (1, BLOCK + RANK), 1)
-
-    both = (high_ref[...], low_ref[...])
-    power = product(split(wt * jnp.where(lane < BLOCK, 1.0, 0.95), 2), both, THREE, NT)
+    weight = jnp.where(lane < BLOCK, 1.0, 0.95)
+    power = product(split(wt * weight, 2), both, THREE, NT)
     ident = identity()
     psp = split(power, 3)
     gram = own_product(power)
-    gpow = product(psp, both, THREE)
-    ritz = own_product(gpow * jnp.where(lane < BLOCK, 1.0, 0.95 ** 0.5))
-    cinv = inverse_root(gram, ident)
+    ritz = []
+
+    def beside(step):
+        if step <= (BLOCK + RANK) // 256:
+            part = pl.ds((step - 1) * 256, 256)
+            gpow = product(psp[:2], (high_ref[:, part], low_ref[:, part]), THREE)
+            all_ref[:, part] = gpow
+            ritz.append(gpow if step <= BLOCK // 256 else gpow * 0.95 ** 0.5)
+
+    cinv = inverse_root(gram, ident, beside)
+    ritz = own_product(jnp.concatenate(ritz, axis=1))
     csp = split(cinv, 3)
     pick_ref[...] = wide_ref[:, block].T
     cols = pick_ref[inner, :]
     pow_ref[...] = power
     rows_ref[...] = pow_ref[:, moved].T
     prow = rows_ref[inner, :]
-    all_ref[...] = gpow
     rows_ref[...] = all_ref[:, block].T
     gcol = rows_ref[inner, :]
     pair = product(split(jnp.concatenate([prow, gcol], axis=0), 3), csp, SIX)
@@ -128,7 +137,13 @@
     fresh_ref[...] = last[:WIDTH]
     middle = jnp.sqrt(eps) * last[WIDTH:] - pair[WIDTH:]
     coef = product(split(middle, 3), csp, SIX)
-    upd_ref[...] = cols + product(split(coef, 3), psp, SIX)
+    update = cols + product(split(coef, 3), psp, SIX)
+    for natural in range(8):
+        ahead, across = natural // 2, natural % 2
+        blocks = [update[:, (4 * side + ahead) * 128:(4 * side + ahead + 1) * 128] for side in (0, 1)]
+        upd_ref[:, natural * 128:(natural + 1) * 128] = jnp.where(
+            place_ref[3] == 0, blocks[across], blocks[1 - across]
+        )
 
 
 def finish(places, both):
@@ -151,7 +166,7 @@
             pltpu.VMEM((128, RANK), jnp.float32),
             pltpu.SemaphoreType.DMA((PARTS,)),
         ],
-        compiler_params=pltpu.CompilerParams(vmem_limit_bytes=48 * 1024 * 1024),
+        compiler_params=pltpu.CompilerParams(vmem_limit_bytes=60 * 1024 * 1024),
     )(places, both)
 
 
@@ -206,16 +221,15 @@
     one, two = groups(True), groups(False)
     band = lax.psum_scatter(part, AXES, scatter_dimension=0, tiled=True, axis_index_groups=one)
     own_sk = lax.ppermute(own_sk, AXES, sketch_moves())
+    own_sk, band = lax.optimization_barrier((own_sk, band))
     rows = jnp.sum(exchange(band.reshape(8, WIDTH, BLOCK), AXES, two), axis=0)
     rows = jnp.concatenate([rows, own_sk], axis=1)
     slab = gather(rows, AXES, 8, two).reshape(8 * WIDTH, BLOCK + RANK)
     both = lax.all_gather(slab, AXES, axis=0, tiled=True, axis_index_groups=one)
     z, y = lax.axis_index("z"), lax.axis_index("y")
-    places = jnp.stack([z, y, (z % 2 + core) % 2 * 4 + z // 2])
+    places = jnp.stack([z, y, (z % 2 + core) % 2 * 4 + z // 2, core])
     update, fresh = finish(places.astype(jnp.int32), both)
-    update = update.reshape(WIDTH, 2, 4, 128)
-    update = jnp.where(core == 0, update, update[:, ::-1])
-    return (update.transpose(2, 1, 3, 0).reshape(1, BLOCK, WIDTH), fresh[None])
+    return (update.T[None], fresh[None])
 
 
 def solution(mesh):

time: 192 us -> 187 us (0.974)
  blocking collectives: 28.2 us -> 46.3 us
  waiting for transfers between devices: 98.5 us -> 80.4 us
  local copies, waits for them, and re-layouts: 4.42 us -> 1.18 us
  starting transfers between devices: 18.9 us -> 16.2 us
    all_to_all x2 -> x3, blocking collectives: 28.2 us -> 46.3 us  [exchange(): lax.all_to_all(parts, axes, split_axis=0, concat_axis=0, tiled=True, axis...]
    reduce_scatter x1, waiting for transfers between devices: 44.2 us -> 34.9 us  [per_device(): lax.psum_scatter(part, AXES, scatter_dimension=0, tiled=True, axis_index_...]
    all_to_all x1 -> x0, waiting for transfers between devices: 6.82 us -> none  [exchange(): lax.all_to_all(parts, axes, split_axis=0, concat_axis=0, tiled=True, axis...]
    all_to_all x1 -> x0, starting transfers between devices: 5.88 us -> none  [exchange(): lax.all_to_all(parts, axes, split_axis=0, concat_axis=0, tiled=True, axis...]
    ppermute x1, starting transfers between devices: 5.26 us -> 8.35 us  [per_device(): own_sk = lax.ppermute(own_sk, AXES, sketch_moves())]
    all_gather x1, waiting for transfers between devices: 46 us -> 43.2 us  [per_device(): both = lax.all_gather(slab, AXES, axis=0, tiled=True, axis_index_groups=one)]
    unnamed x7 -> x5, local copies, waits for them, and re-layouts: 3.58 us -> 1.1 us
  transfers between devices with their start and end apart: 5 -> 4, of which waited for: 4 -> 4; matrix products, arithmetic and copies ran while one was open for 0% -> 0% of each run, Pallas kernels for 0% -> 0%
where the time goes in v3:
time: 187 us; the launch traced here: 185 us
  waiting for transfers between devices  80.4 us (43%)
  blocking collectives  46.3 us (25%)
  Pallas kernels  23.3 us (12%)
  starting transfers between devices  16.2 us (9%)
  between operations  14.2 us (8%)
  matrix products  3.19 us (2%)
    all_to_all x3, blocking collectives, exchange(): lax.all_to_all(parts, axes, split_axis=0, concat_axis=0, tiled=True, axis...  46.3 us
    all_gather x1, waiting for transfers between devices, per_device(): both = lax.all_gather(slab, AXES, axis=0, tiled=True, axis_index_groups=one)  43.2 us
    reduce_scatter x1, waiting for transfers between devices, per_device(): lax.psum_scatter(part, AXES, scatter_dimension=0, tiled=True, axis_index_...  34.9 us
    pallas_call x1, Pallas kernels, finish(): pl.pallas_call(finish_kernel, out_shape=(jax.ShapeDtypeStruct((WIDTH, BLO...  23.3 us
    ppermute x1, starting transfers between devices, per_device(): own_sk = lax.ppermute(own_sk, AXES, sketch_moves())  8.35 us
    ppermute x1, starting transfers between devices, per_device(): far = lax.ppermute(near, 'core', [(0, 1), (1, 0)])  7.81 us
  transfers between devices with their start and end apart: 4, of which 4 were waited for; matrix products, arithmetic and copies ran while one was open for 0% of the time, Pallas kernels for 0%

profile of v3, /device:TPU:1, one launch (start us, length us, event | category | flops | bytes accessed | tf_op | source)
XLA Modules:
  0.0 185.4 jit_solution(11526144140526370404)
XLA Ops:
  7.2 0.0 copy-start
  7.2 0.0 reduce-scatter.2.cloned.1.call-start
  7.2 1.1 copy.5
  8.4 11.6 %all_to_all.15 = bf16[4,512,128]{1,2,0:T(8,128)(2,1)S(1)} all-to-all(bf16[4,512,128]{1,2,0:T(8,128)(2,1)S(1)} %broadcast_in_dim.8), channel_id=1, replica_groups=mesh['z'=8,'y'=8,'x'=4,'core'=2] {'x'}, dimensions={0} | all-to-all | bytes 1048576 | tf_op jit(solution)/shard_map/all_to_all | solution.py:201
  19.9 0.0 copy-start.1
  19.9 7.8 %collective-permute-start = (bf16[4,512,128]{1,2,0:T(8,128)(2,1)S(1)}, bf16[4,512,128]{1,2,0:T(8,128)(2,1)S(1)}, u32[]{:S(2)}, u32[]{:S(2)}) collective-permute-start(bf16[4,512,128]{1,2,0:T(8,128)(2,1)S(1)} %all_to_all.15), channel_id=1, source_target_pairs={{0,1},{1,0},{2,3},{3,2},{4,5},{5,4},{6,7},{7,6},{8,9},{9,8},{10,11... | collective-permute-start | bytes 1572872 | tf_op jit(solution)/shard_map/ppermute | solution.py:212
  27.8 1.5 collective-permute-done
  29.3 0.0 copy-done
  29.3 3.2 %fusion = f32[8,128,1024]{2,1,0:T(8,128)} fusion(bf16[4,512,128]{1,2,0:T(8,128)(2,1)S(1)} %collective-permute-done, bf16[4,512,128]{1,2,0:T(8,128)(2,1)S(1)} %all_to_all.15, bf16[512,1024]{1,0:T(8,128)(2,1)S(1)} %copy-done), kind=kOutput, calls=%fused_computation | convolution fusion | flops 1074266112 | bytes 6291456 | tf_op jit(solution)/shard_map/dot_general | solution.py:214
  32.5 0.0 reduce-scatter.2.cloned.1.call-update
  32.5 0.0 all-gather.2.cloned.1.call-start
  32.5 0.0 copy-done.1
  32.6 8.4 %collective-permute-start.1 = (f32[16,256]{1,0:T(8,128)S(1)}, f32[16,256]{1,0:T(8,128)S(1)}, u32[]{:S(2)}, u32[]{:S(2)}) collective-permute-start(f32[16,256]{1,0:T(8,128)S(1)} %bitcast.19), channel_id=1, source_target_pairs={{0,0},{65,1},{2,2},{67,3},{4,4},{69,5},{6,6},{71,7},{128,8},{73,9}... | collective-permute-start | bytes 49160 | tf_op jit(solution)/shard_map/ppermute | solution.py:223
  40.9 0.8 collective-permute-done.1
  41.8 34.9 %reduce-scatter.2.cloned.1.call-done = f32[128,1024]{1,0:T(8,128)} async-done(((f32[1024,1024]{1,0:T(8,128)}), f32[128,1024]{1,0:T(8,128)}) %reduce-scatter.2.cloned.1.call-update) | async-done | bytes 524304 | tf_op jit(solution)/shard_map/reduce_scatter | solution.py:222
  76.6 18.0 %all_to_all.16 = f32[8,16,1024]{2,1,0:T(8,128)S(1)} all-to-all(f32[8,16,1024]{2,1,0:T(8,128)} %bitcast.17), channel_id=1, replica_groups={{0,64,128,192,256,320,384,448},{1,9,17,25,33,41,49,57},{8,72,136,200,26..., dimensions={0} | all-to-all | bytes 1048576 | tf_op jit(solution)/shard_map/all_to_all | solution.py:201
  94.8 16.6 %all_to_all.17 = f32[8,16,1280]{2,1,0:T(8,128)} all-to-all(f32[8,16,1280]{2,1,0:T(8,128)S(1)} %broadcast_in_dim.9), channel_id=1, replica_groups={{0,64,128,192,256,320,384,448},{1,9,17,25,33,41,49,57},{8,72,136,200,26..., dimensions={0} | all-to-all | bytes 1310720 | tf_op jit(solution)/shard_map/all_to_all | solution.py:201
  111.4 0.0 all-gather.2.cloned.1.call-update
  111.5 0.6 pad_add_fusion.place_ref
  112.1 43.2 %all-gather.2.cloned.1.call-done.both_ref = f32[1024,1280]{1,0:T(8,128)} async-done(((f32[128,1280]{1,0:T(8,128)}), f32[1024,1280]{1,0:T(8,128)}) %all-gather.2.cloned.1.call-update) | async-done | bytes 5242896 | tf_op jit(solution)/shard_map/all_gather | solution.py:228
  155.3 23.3 %shard_map.50 = (f32[16,1024]{1,0:T(8,128)}, f32[16,256]{1,0:T(8,128)}) custom-call(s32[4]{0:T(128)} %pad_add_fusion.place_ref, f32[1024,1280]{1,0:T(8,128)} %all-gather.2.cloned.1.call-done.both_ref), custom_call_target="tpu_custom_call" | custom-call | tf_op jit(solution)/shard_map/pallas_call | solution.py:151
  (4 shorter events, 0.1 us)
Async XLA Ops:
  7.2 22.1 %copy-start = (bf16[512,1024]{1,0:T(8,128)(2,1)S(1)}, bf16[512,1024]{1,0:T(8,128)(2,1)}, u32[]{:S(2)}) copy-start(bf16[512,1024]{1,0:T(8,128)(2,1)} %param.4) | copy-start | bytes 3145732
  7.2 69.5 %reduce-scatter.2.cloned.1.call-start = ((), (), s32[]{:S(2)}) async-start(), calls=%async_computation.4 | async-start | bytes 4718592 | tf_op jit(solution)/shard_map/reduce_scatter | solution.py:222
  19.9 12.6 %copy-start.1 = (f32[1,16,256]{2,1,0:T(8,128)S(1)}, f32[1,16,256]{2,1,0:T(8,128)}, u32[]{:S(2)}) copy-start(f32[1,16,256]{2,1,0:T(8,128)} %param.5) | copy-start | bytes 49156
  19.9 9.3 %collective-permute-start = (bf16[4,512,128]{1,2,0:T(8,128)(2,1)S(1)}, bf16[4,512,128]{1,2,0:T(8,128)(2,1)S(1)}, u32[]{:S(2)}, u32[]{:S(2)}) collective-permute-start(bf16[4,512,128]{1,2,0:T(8,128)(2,1)S(1)} %all_to_all.15), channel_id=1, source_target_pairs={{0,1},{1,0},{2,3},{3,2},{4,5},{5,4},{6,7},{7,6},{8,9},{9,8},{10,11... | collective-permute-start | bytes 1572872 | tf_op jit(solution)/shard_map/ppermute | solution.py:212
  32.5 122.8 %all-gather.2.cloned.1.call-start = ((), (), s32[]{:S(2)}) async-start(), calls=%async_computation.5 | async-start | bytes 5898240 | tf_op jit(solution)/shard_map/all_gather | solution.py:228
  32.6 9.2 %collective-permute-start.1 = (f32[16,256]{1,0:T(8,128)S(1)}, f32[16,256]{1,0:T(8,128)S(1)}, u32[]{:S(2)}, u32[]{:S(2)}) collective-permute-start(f32[16,256]{1,0:T(8,128)S(1)} %bitcast.19), channel_id=1, source_target_pairs={{0,0},{65,1},{2,2},{67,3},{4,4},{69,5},{6,6},{71,7},{128,8},{73,9}... | collective-permute-start | bytes 49160 | tf_op jit(solution)/shard_map/ppermute | solution.py:223
Sparse Core Ops, SparseCore 0:
  32.6 43.9 reduce-scatter.1
  111.6 43.6 all-gather.1

commit v4 on v3

--- a/solution.py
+++ b/solution.py
@@ -19,6 +19,10 @@
 
 THREE = ((0, 1), (1, 0), (0, 0))
 SIX = ((1, 1), (2, 0), (0, 2), (0, 1), (1, 0), (0, 0))
+
+
+def matmul(left, right):
+    return jnp.dot(left, right, precision=lax.Precision.HIGHEST, preferred_element_type=jnp.float32)
 
 
 def split(value, count):
@@ -79,14 +83,15 @@
 
 
 def finish_kernel(
-    place_ref, both_ref, upd_ref, fresh_ref,
+    place_ref, grad_ref, skt_ref, base_ref, upd_ref, fresh_ref,
     wide_ref, high_ref, low_ref, all_ref, pow_ref, pick_ref, rows_ref, sems,
 ):
     copies = []
     for part in range(PARTS):
         band = pl.ds(part * BAND, BAND)
-        copies.append(pltpu.make_async_copy(both_ref.at[band, :], wide_ref.at[band, :], sems.at[part]))
+        copies.append(pltpu.make_async_copy(grad_ref.at[band, :], wide_ref.at[band, :], sems.at[part]))
         copies[-1].start()
+    ssp = split(skt_ref[...], 2)
     wt = None
     for part in range(PARTS):
         copies[part].wait()
@@ -94,28 +99,28 @@
         high, low = split(wide_ref[band, :], 2)
         high_ref[band, :] = high
         low_ref[band, :] = low
-        skt = wide_ref[band, BLOCK:].T
-        term = product(split(skt, 2), (high, low), THREE)
+        own = [piece[:, part * BAND:(part + 1) * BAND] for piece in ssp]
+        term = product(own, (high, low), THREE)
         wt = term if wt is None else wt + term
     block = pl.ds(pl.multiple_of(place_ref[0] * 128, 128), 128)
     inner = pl.ds(pl.multiple_of(place_ref[1] * WIDTH, WIDTH), WIDTH)
     moved = pl.ds(pl.multiple_of(place_ref[2] * 128, 128), 128)
 
     both = (high_ref[...], low_ref[...])
-    lane = lax.broadcasted_iota(jnp.int32, (1, BLOCK + RANK), 1)
-    weight = jnp.where(lane < BLOCK, 1.0, 0.95)
-    power = product(split(wt * weight, 2), both, THREE, NT)
+    power = base_ref[...] + product(split(wt, 2), both, THREE, NT)
     ident = identity()
     psp = split(power, 3)
     gram = own_product(power)
     ritz = []
 
     def beside(step):
-        if step <= (BLOCK + RANK) // 256:
+        if step <= BLOCK // 256:
             part = pl.ds((step - 1) * 256, 256)
             gpow = product(psp[:2], (high_ref[:, part], low_ref[:, part]), THREE)
             all_ref[:, part] = gpow
-            ritz.append(gpow if step <= BLOCK // 256 else gpow * 0.95 ** 0.5)
+            ritz.append(gpow)
+        elif step == BLOCK // 256 + 1:
+            ritz.append(product(psp[:2], ssp, THREE, NT) * 0.95 ** 0.5)
 
     cinv = inverse_root(gram, ident, beside)
     ritz = own_product(jnp.concatenate(ritz, axis=1))
@@ -146,7 +151,7 @@
         )
 
 
-def finish(places, both):
+def finish(places, grad, skt, base):
     whole = pl.BlockSpec(memory_space=pltpu.VMEM)
     return pl.pallas_call(
         finish_kernel,
@@ -154,20 +159,25 @@
             jax.ShapeDtypeStruct((WIDTH, BLOCK), jnp.float32),
             jax.ShapeDtypeStruct((WIDTH, RANK), jnp.float32),
         ),
-        in_specs=[pl.BlockSpec(memory_space=pltpu.SMEM), pl.BlockSpec(memory_space=pltpu.HBM)],
+        in_specs=[
+            pl.BlockSpec(memory_space=pltpu.SMEM),
+            pl.BlockSpec(memory_space=pltpu.HBM),
+            whole,
+            whole,
+        ],
         out_specs=(whole, whole),
         scratch_shapes=[
-            pltpu.VMEM((BLOCK, BLOCK + RANK), jnp.float32),
-            pltpu.VMEM((BLOCK, BLOCK + RANK), jnp.bfloat16),
-            pltpu.VMEM((BLOCK, BLOCK + RANK), jnp.bfloat16),
-            pltpu.VMEM((RANK, BLOCK + RANK), jnp.float32),
+            pltpu.VMEM((BLOCK, BLOCK), jnp.float32),
+            pltpu.VMEM((BLOCK, BLOCK), jnp.bfloat16),
+            pltpu.VMEM((BLOCK, BLOCK), jnp.bfloat16),
+            pltpu.VMEM((RANK, BLOCK), jnp.float32),
             pltpu.VMEM((RANK, BLOCK), jnp.float32),
             pltpu.VMEM((128, BLOCK), jnp.float32),
             pltpu.VMEM((128, RANK), jnp.float32),
             pltpu.SemaphoreType.DMA((PARTS,)),
         ],
-        compiler_params=pltpu.CompilerParams(vmem_limit_bytes=60 * 1024 * 1024),
-    )(places, both)
+        compiler_params=pltpu.CompilerParams(vmem_limit_bytes=57 * 1024 * 1024),
+    )(places, grad, skt, base)
 
 
 def groups(first):
@@ -181,20 +191,6 @@
                     for i in range(8)
                 ])
     return sets
-
-
-def sketch_moves():
-    nz, ny, nx, nc = SIZES
-    moves = []
-    for z in range(nz):
-        for y in range(ny):
-            for x in range(nx):
-                for core in range(nc):
-                    position, inner = (y, z) if core == 0 else (z, y)
-                    natural = position % 4 * 2 + (position // 4 + core) % 2
-                    source = ((natural * ny + inner) * nx + x) * nc + core
-                    moves.append((source, ((z * ny + y) * nx + x) * nc + core))
-    return moves
 
 
 def exchange(parts, axes, sets=None):
@@ -220,15 +216,21 @@
     part, own_sk = lax.optimization_barrier((part, sketch[0]))
     one, two = groups(True), groups(False)
     band = lax.psum_scatter(part, AXES, scatter_dimension=0, tiled=True, axis_index_groups=one)
-    own_sk = lax.ppermute(own_sk, AXES, sketch_moves())
-    own_sk, band = lax.optimization_barrier((own_sk, band))
+    sk = gather(own_sk, AXES, 8, one).reshape(8 * WIDTH, RANK)
+    sk = gather(sk, AXES, 8, two)
+    sk, band = lax.optimization_barrier((sk, band))
     rows = jnp.sum(exchange(band.reshape(8, WIDTH, BLOCK), AXES, two), axis=0)
-    rows = jnp.concatenate([rows, own_sk], axis=1)
-    slab = gather(rows, AXES, 8, two).reshape(8 * WIDTH, BLOCK + RANK)
-    both = lax.all_gather(slab, AXES, axis=0, tiled=True, axis_index_groups=one)
+    slab = gather(rows, AXES, 8, two).reshape(8 * WIDTH, BLOCK)
+    grad = lax.all_gather(slab, AXES, axis=0, tiled=True, axis_index_groups=one)
+
+    sk = sk.reshape(8, 8, WIDTH, RANK)
+    sk = jnp.where(core == 0, sk, sk.swapaxes(0, 1)).reshape(4, 2, 128, RANK).swapaxes(0, 1)
+    sk = jnp.where(core == 0, sk, sk[::-1]).reshape(BLOCK, RANK)
+    skt = sk.T
+    base = 0.95 * matmul(matmul(skt, sk), skt)
     z, y = lax.axis_index("z"), lax.axis_index("y")
     places = jnp.stack([z, y, (z % 2 + core) % 2 * 4 + z // 2, core])
-    update, fresh = finish(places.astype(jnp.int32), both)
+    update, fresh = finish(places.astype(jnp.int32), grad, skt, base)
     return (update.T[None], fresh[None])
 
 

time: 187 us -> 192 us (1.027)
  blocking collectives: 46.3 us -> 90.7 us
  waiting for transfers between devices: 80.4 us -> 43.4 us
  starting transfers between devices: 16.2 us -> 7.89 us
  matrix products: 3.19 us -> 7.06 us
  local copies, waits for them, and re-layouts: 1.18 us -> 4.24 us
    all_to_all x3 -> x5, blocking collectives: 46.3 us -> 90.7 us  [exchange(): lax.all_to_all(parts, axes, split_axis=0, concat_axis=0, tiled=True, axis...]
    reduce_scatter x1, waiting for transfers between devices: 34.9 us -> 7.63 us  [per_device(): lax.psum_scatter(part, AXES, scatter_dimension=0, tiled=True, axis_index_...]
    all_gather x1, waiting for transfers between devices: 43.2 us -> 34.2 us  [per_device(): grad = lax.all_gather(slab, AXES, axis=0, tiled=True, axis_index_groups=one)]
    ppermute x1 -> x0, starting transfers between devices: 8.35 us -> none  [per_device(): own_sk = lax.ppermute(own_sk, AXES, sketch_moves())]
    dot_general x0 -> x2, matrix products: none -> 3.88 us  [matmul(): jnp.dot(left, right, precision=lax.Precision.HIGHEST, preferred_element_t...]
  transfers between devices with their start and end apart: 4 -> 3, of which waited for: 4 -> 3; matrix products, arithmetic and copies ran while one was open for 0% -> 4% of each run, Pallas kernels for 0% -> 0%
where the time goes in v4:
time: 192 us; the launch traced here: 190 us
  blocking collectives  90.7 us (47%)
  waiting for transfers between devices  43.4 us (23%)
  Pallas kernels  21.4 us (11%)
  between operations  14.2 us (7%)
  starting transfers between devices  7.89 us (4%)
  matrix products  7.06 us (4%)
  local copies, waits for them, and re-layouts  4.24 us (2%)
    all_to_all x5, blocking collectives, exchange(): lax.all_to_all(parts, axes, split_axis=0, concat_axis=0, tiled=True, axis...  90.7 us
    all_gather x1, waiting for transfers between devices, per_device(): grad = lax.all_gather(slab, AXES, axis=0, tiled=True, axis_index_groups=one)  34.2 us
    pallas_call x1, Pallas kernels, finish(): pl.pallas_call(finish_kernel, out_shape=(jax.ShapeDtypeStruct((WIDTH, BLO...  21.4 us
    ppermute x1, starting transfers between devices, per_device(): far = lax.ppermute(near, 'core', [(0, 1), (1, 0)])  7.81 us
    reduce_scatter x1, waiting for transfers between devices, per_device(): lax.psum_scatter(part, AXES, scatter_dimension=0, tiled=True, axis_index_...  7.63 us
    dot_general x2, matrix products, matmul(): jnp.dot(left, right, precision=lax.Precision.HIGHEST, preferred_element_t...  3.88 us
  transfers between devices with their start and end apart: 3, of which 3 were waited for; matrix products, arithmetic and copies ran while one was open for 4% of the time, Pallas kernels for 0%

profile of v4, /device:TPU:1, one launch (start us, length us, event | category | flops | bytes accessed | tf_op | source)
XLA Modules:
  0.0 189.8 jit_solution(17637503955503621582)
XLA Ops:
  7.2 0.0 copy-start
  7.2 0.0 reduce-scatter.2.cloned.1.call-start
  7.2 1.1 copy.10
  8.4 11.6 %all_to_all.25 = bf16[4,512,128]{1,2,0:T(8,128)(2,1)S(1)} all-to-all(bf16[4,512,128]{1,2,0:T(8,128)(2,1)S(1)} %broadcast_in_dim.14), channel_id=1, replica_groups=mesh['z'=8,'y'=8,'x'=4,'core'=2] {'x'}, dimensions={0} | all-to-all | bytes 1048576 | tf_op jit(solution)/shard_map/all_to_all | solution.py:197
  19.9 0.0 copy-start.2
  19.9 7.8 %collective-permute-start = (bf16[4,512,128]{1,2,0:T(8,128)(2,1)S(1)}, bf16[4,512,128]{1,2,0:T(8,128)(2,1)S(1)}, u32[]{:S(2)}, u32[]{:S(2)}) collective-permute-start(bf16[4,512,128]{1,2,0:T(8,128)(2,1)S(1)} %all_to_all.25), channel_id=1, source_target_pairs={{0,1},{1,0},{2,3},{3,2},{4,5},{5,4},{6,7},{7,6},{8,9},{9,8},{10,11... | collective-permute-start | bytes 1572872 | tf_op jit(solution)/shard_map/ppermute | solution.py:208
  27.8 1.5 collective-permute-done
  29.3 0.0 copy-done
  29.3 3.2 %fusion = f32[8,128,1024]{2,1,0:T(8,128)} fusion(bf16[4,512,128]{1,2,0:T(8,128)(2,1)S(1)} %collective-permute-done, bf16[4,512,128]{1,2,0:T(8,128)(2,1)S(1)} %all_to_all.25, bf16[512,1024]{1,0:T(8,128)(2,1)S(1)} %copy-done), kind=kOutput, calls=%fused_computation.3 | convolution fusion | flops 1074266112 | bytes 6291456 | tf_op jit(solution)/shard_map/dot_general | solution.py:210
  32.5 0.0 reduce-scatter.2.cloned.1.call-update
  32.5 0.0 all-gather.2.cloned.1.call-start
  32.5 0.0 copy-done.2
  32.6 15.5 %all_to_all.26 = f32[8,16,256]{2,1,0:T(8,128)S(1)} all-to-all(f32[8,16,256]{2,1,0:T(8,128)S(1)} %broadcast_in_dim.15), channel_id=1, replica_groups={{0,8,16,24,32,40,48,56},{1,65,129,193,257,321,385,449},{64,72,80,88,96,..., dimensions={0} | all-to-all | bytes 262144 | tf_op jit(solution)/shard_map/all_to_all | solution.py:197
  48.0 0.1 broadcast_in_dim.34
  48.1 29.9 %all_to_all.27 = f32[8,128,256]{2,1,0:T(8,128)S(1)} all-to-all(f32[8,128,256]{2,1,0:T(8,128)S(1)} %broadcast_in_dim.34), channel_id=1, replica_groups={{0,64,128,192,256,320,384,448},{1,9,17,25,33,41,49,57},{8,72,136,200,26..., dimensions={0} | all-to-all | bytes 2097152 | tf_op jit(solution)/shard_map/all_to_all | solution.py:197
  78.0 7.6 %reduce-scatter.2.cloned.1.call-done = f32[128,1024]{1,0:T(8,128)} async-done(((f32[1024,1024]{1,0:T(8,128)}), f32[128,1024]{1,0:T(8,128)}) %reduce-scatter.2.cloned.1.call-update) | async-done | bytes 524304 | tf_op jit(solution)/shard_map/reduce_scatter | solution.py:218
  85.7 18.5 %all_to_all.28 = f32[8,16,1024]{2,1,0:T(8,128)S(1)} all-to-all(f32[8,16,1024]{2,1,0:T(8,128)} %bitcast.37), channel_id=1, replica_groups={{0,64,128,192,256,320,384,448},{1,9,17,25,33,41,49,57},{8,72,136,200,26..., dimensions={0} | all-to-all | bytes 1048576 | tf_op jit(solution)/shard_map/all_to_all | solution.py:197
  104.3 15.2 %all_to_all.29 = f32[8,16,1024]{2,1,0:T(8,128)} all-to-all(f32[8,16,1024]{2,1,0:T(8,128)S(1)} %broadcast_in_dim.35), channel_id=1, replica_groups={{0,64,128,192,256,320,384,448},{1,9,17,25,33,41,49,57},{8,72,136,200,26..., dimensions={0} | all-to-all | bytes 1048576 | tf_op jit(solution)/shard_map/all_to_all | solution.py:197
  119.5 0.0 all-gather.2.cloned.1.call-update
  119.6 0.7 pad_add_fusion.place_ref
  120.2 0.1 bitcast_select_fusion
  120.4 0.1 reverse_select_fusion
  120.5 1.3 copy.12
  121.8 1.6 reshape.31
  123.4 0.0 copy-start.1
  123.4 1.8 convolution_bitcast_fusion
  125.3 2.0 %convolution_multiply_fusion.base_ref = f32[256,1024]{1,0:T(8,128)} fusion(f32[256,256]{1,0:T(8,128)S(1)} %convolution_bitcast_fusion, f32[1024,256]{0,1:T(8,128)S(1)} %reshape.31), kind=kOutput, calls=%fused_computation.1 | convolution fusion | flops 805568512 | bytes 2359296 | tf_op jit(solution)/shard_map/dot_general | solution.py:25
  127.3 34.2 %all-gather.2.cloned.1.call-done.grad_ref = f32[1024,1024]{1,0:T(8,128)} async-done(((f32[128,1024]{1,0:T(8,128)}), f32[1024,1024]{1,0:T(8,128)}) %all-gather.2.cloned.1.call-update) | async-done | bytes 4194320 | tf_op jit(solution)/shard_map/all_gather | solution.py:224
  161.5 0.0 copy-done.1
  161.6 21.4 %shard_map.50 = (f32[16,1024]{1,0:T(8,128)}, f32[16,256]{1,0:T(8,128)}) custom-call(s32[4]{0:T(128)} %pad_add_fusion.place_ref, f32[1024,1024]{1,0:T(8,128)} %all-gather.2.cloned.1.call-done.grad_ref, f32[256,1024]{1,0:T(8,128)} %bitcast.32, f32[256,1024]{1,0:T(8,128)} %convolution_multiply_fusion.base_ref), custom_call_target="tpu_custom_call" | custom-call | tf_op jit(solution)/shard_map/pallas_call | solution.py:156
  (4 shorter events, 0.1 us)
Async XLA Ops:
  7.2 22.1 %copy-start = (bf16[512,1024]{1,0:T(8,128)(2,1)S(1)}, bf16[512,1024]{1,0:T(8,128)(2,1)}, u32[]{:S(2)}) copy-start(bf16[512,1024]{1,0:T(8,128)(2,1)} %param.4) | copy-start | bytes 3145732
  7.2 78.5 %reduce-scatter.2.cloned.1.call-start = ((), (), s32[]{:S(2)}) async-start(), calls=%async_computation.6 | async-start | bytes 4718592 | tf_op jit(solution)/shard_map/reduce_scatter | solution.py:218
  19.9 12.6 %copy-start.2 = (f32[1,16,256]{2,1,0:T(8,128)S(1)}, f32[1,16,256]{2,1,0:T(8,128)}, u32[]{:S(2)}) copy-start(f32[1,16,256]{2,1,0:T(8,128)} %param.5) | copy-start | bytes 49156
  19.9 9.3 %collective-permute-start = (bf16[4,512,128]{1,2,0:T(8,128)(2,1)S(1)}, bf16[4,512,128]{1,2,0:T(8,128)(2,1)S(1)}, u32[]{:S(2)}, u32[]{:S(2)}) collective-permute-start(bf16[4,512,128]{1,2,0:T(8,128)(2,1)S(1)} %all_to_all.25), channel_id=1, source_target_pairs={{0,1},{1,0},{2,3},{3,2},{4,5},{5,4},{6,7},{7,6},{8,9},{9,8},{10,11... | collective-permute-start | bytes 1572872 | tf_op jit(solution)/shard_map/ppermute | solution.py:208
  32.5 129.1 %all-gather.2.cloned.1.call-start = ((), (), s32[]{:S(2)}) async-start(), calls=%async_computation.7 | async-start | bytes 4718592 | tf_op jit(solution)/shard_map/all_gather | solution.py:224
  123.4 38.1 %copy-start.1 = (f32[1024,256]{0,1:T(8,128)}, f32[1024,256]{0,1:T(8,128)S(1)}, u32[]{:S(2)}) copy-start(f32[1024,256]{0,1:T(8,128)S(1)} %reshape.31) | copy-start | bytes 3145732
Sparse Core Ops, SparseCore 0:
  32.6 53.0 reduce-scatter.1
  119.7 41.8 all-gather.1

commit v5 on v4

--- a/solution.py
+++ b/solution.py
@@ -78,8 +78,18 @@
     return zmat * lax.rsqrt(scale)
 
 
-def full_product(left, right):
-    return product(split(left, 3), split(right, 3), SIX)
+def few_rows(left, right):
+    one, two, three = split(left, 3)
+    rows = left.shape[0]
+    first = lax.dot_general(
+        jnp.concatenate([three, two, one]), right[0], NN, preferred_element_type=jnp.float32
+    )
+    second = lax.dot_general(
+        jnp.concatenate([two, one]), right[1], NN, preferred_element_type=jnp.float32
+    )
+    third = lax.dot_general(one, right[2], NN, preferred_element_type=jnp.float32)
+    low = second[:rows] + third + first[:rows]
+    return low + (second[rows:] + first[rows:2 * rows]) + first[2 * rows:]
 
 
 def finish_kernel(
@@ -132,17 +142,24 @@
     prow = rows_ref[inner, :]
     rows_ref[...] = all_ref[:, block].T
     gcol = rows_ref[inner, :]
-    pair = product(split(jnp.concatenate([prow, gcol], axis=0), 3), csp, SIX)
     hmat = product(split(product(csp, split(ritz, 3), SIX), 3), csp, SIX)
     eps = trace(hmat, ident) * (0.1 / RANK)
     hdamp = hmat + eps * ident
-    lead = full_product(pair[:WIDTH], hdamp)
-    rinv = inverse_root(hdamp, ident)
-    last = full_product(jnp.concatenate([lead, pair[WIDTH:]], axis=0), rinv)
+    held = []
+
+    def late(step):
+        if step == 1:
+            held.append(few_rows(jnp.concatenate([prow, gcol], axis=0), csp))
+        if step == 2:
+            held.append(few_rows(held[0][:WIDTH], split(hdamp, 3)))
+
+    rinv = inverse_root(hdamp, ident, late)
+    pair, lead = held
+    last = few_rows(jnp.concatenate([lead, pair[WIDTH:]], axis=0), split(rinv, 3))
     fresh_ref[...] = last[:WIDTH]
     middle = jnp.sqrt(eps) * last[WIDTH:] - pair[WIDTH:]
-    coef = product(split(middle, 3), csp, SIX)
-    update = cols + product(split(coef, 3), psp, SIX)
+    coef = few_rows(middle, csp)
+    update = cols + few_rows(coef, psp)
     for natural in range(8):
         ahead, across = natural // 2, natural % 2
         blocks = [update[:, (4 * side + ahead) * 128:(4 * side + ahead + 1) * 128] for side in (0, 1)]
@@ -217,12 +234,12 @@
     one, two = groups(True), groups(False)
     band = lax.psum_scatter(part, AXES, scatter_dimension=0, tiled=True, axis_index_groups=one)
     sk = gather(own_sk, AXES, 8, one).reshape(8 * WIDTH, RANK)
-    sk = gather(sk, AXES, 8, two)
     sk, band = lax.optimization_barrier((sk, band))
     rows = jnp.sum(exchange(band.reshape(8, WIDTH, BLOCK), AXES, two), axis=0)
     slab = gather(rows, AXES, 8, two).reshape(8 * WIDTH, BLOCK)
     grad = lax.all_gather(slab, AXES, axis=0, tiled=True, axis_index_groups=one)
 
+    sk = gather(sk, AXES, 8, two)
     sk = sk.reshape(8, 8, WIDTH, RANK)
     sk = jnp.where(core == 0, sk, sk.swapaxes(0, 1)).reshape(4, 2, 128, RANK).swapaxes(0, 1)
     sk = jnp.where(core == 0, sk, sk[::-1]).reshape(BLOCK, RANK)

time: 192 us -> 189 us (0.984)
  blocking collectives: 90.7 us -> 60.2 us
  waiting for transfers between devices: 43.4 us -> 68.2 us
  starting transfers between devices: 7.89 us -> 11.6 us
    all_to_all x5 -> x4, blocking collectives: 90.7 us -> 60.2 us  [exchange(): lax.all_to_all(parts, axes, split_axis=0, concat_axis=0, tiled=True, axis...]
    reduce_scatter x1, waiting for transfers between devices: 7.63 us -> 28.8 us  [per_device(): lax.psum_scatter(part, AXES, scatter_dimension=0, tiled=True, axis_index_...]
    all_to_all x0 -> x1, waiting for transfers between devices: none -> 17.5 us  [exchange(): lax.all_to_all(parts, axes, split_axis=0, concat_axis=0, tiled=True, axis...]
    all_gather x1, waiting for transfers between devices: 34.2 us -> 20.4 us  [per_device(): grad = lax.all_gather(slab, AXES, axis=0, tiled=True, axis_index_groups=one)]
    all_to_all x0 -> x1, starting transfers between devices: none -> 3.74 us  [exchange(): lax.all_to_all(parts, axes, split_axis=0, concat_axis=0, tiled=True, axis...]
  transfers between devices with their start and end apart: 3 -> 4, of which waited for: 3 -> 4; matrix products, arithmetic and copies ran while one was open for 4% -> 5% of each run, Pallas kernels for 0% -> 0%
where the time goes in v5:
time: 189 us; the launch traced here: 188 us
  waiting for transfers between devices  68.2 us (36%)
  blocking collectives  60.2 us (32%)
  Pallas kernels  21.1 us (11%)
  between operations  14.2 us (8%)
  starting transfers between devices  11.6 us (6%)
  matrix products  7.08 us (4%)
  local copies, waits for them, and re-layouts  5.23 us (3%)
    all_to_all x4, blocking collectives, exchange(): lax.all_to_all(parts, axes, split_axis=0, concat_axis=0, tiled=True, axis...  60.2 us
    reduce_scatter x1, waiting for transfers between devices, per_device(): lax.psum_scatter(part, AXES, scatter_dimension=0, tiled=True, axis_index_...  28.8 us
    pallas_call x1, Pallas kernels, finish(): pl.pallas_call(finish_kernel, out_shape=(jax.ShapeDtypeStruct((WIDTH, BLO...  21.1 us
    all_gather x1, waiting for transfers between devices, per_device(): grad = lax.all_gather(slab, AXES, axis=0, tiled=True, axis_index_groups=one)  20.4 us
    all_to_all x1, waiting for transfers between devices, exchange(): lax.all_to_all(parts, axes, split_axis=0, concat_axis=0, tiled=True, axis...  17.5 us
    ppermute x1, starting transfers between devices, per_device(): far = lax.ppermute(near, 'core', [(0, 1), (1, 0)])  7.81 us
    dot_general x2, matrix products, matmul(): jnp.dot(left, right, precision=lax.Precision.HIGHEST, preferred_element_t...  3.88 us
  transfers between devices with their start and end apart: 4, of which 4 were waited for; matrix products, arithmetic and copies ran while one was open for 5% of the time, Pallas kernels for 0%

profile of v5, /device:TPU:1, one launch (start us, length us, event | category | flops | bytes accessed | tf_op | source)
XLA Modules:
  0.0 188.5 jit_solution(6157791464322937068)
XLA Ops:
  7.2 0.0 copy-start
  7.2 0.0 reduce-scatter.2.cloned.1.call-start
  7.2 1.1 copy.7
  8.4 11.6 %all_to_all.25 = bf16[4,512,128]{1,2,0:T(8,128)(2,1)S(1)} all-to-all(bf16[4,512,128]{1,2,0:T(8,128)(2,1)S(1)} %broadcast_in_dim.12), channel_id=1, replica_groups=mesh['z'=8,'y'=8,'x'=4,'core'=2] {'x'}, dimensions={0} | all-to-all | bytes 1048576 | tf_op jit(solution)/shard_map/all_to_all | solution.py:214
  19.9 0.0 copy-start.2
  19.9 7.8 %collective-permute-start = (bf16[4,512,128]{1,2,0:T(8,128)(2,1)S(1)}, bf16[4,512,128]{1,2,0:T(8,128)(2,1)S(1)}, u32[]{:S(2)}, u32[]{:S(2)}) collective-permute-start(bf16[4,512,128]{1,2,0:T(8,128)(2,1)S(1)} %all_to_all.25), channel_id=1, source_target_pairs={{0,1},{1,0},{2,3},{3,2},{4,5},{5,4},{6,7},{7,6},{8,9},{9,8},{10,11... | collective-permute-start | bytes 1572872 | tf_op jit(solution)/shard_map/ppermute | solution.py:225
  27.8 1.5 collective-permute-done
  29.3 0.0 copy-done
  29.3 3.2 %fusion = f32[8,128,1024]{2,1,0:T(8,128)} fusion(bf16[4,512,128]{1,2,0:T(8,128)(2,1)S(1)} %collective-permute-done, bf16[4,512,128]{1,2,0:T(8,128)(2,1)S(1)} %all_to_all.25, bf16[512,1024]{1,0:T(8,128)(2,1)S(1)} %copy-done), kind=kOutput, calls=%fused_computation.3 | convolution fusion | flops 1074266112 | bytes 6291456 | tf_op jit(solution)/shard_map/dot_general | solution.py:227
  32.5 0.0 reduce-scatter.2.cloned.1.call-update
  32.5 0.0 all-gather.2.cloned.1.call-start
  32.6 0.0 copy-done.2
  32.6 15.5 %all_to_all.26 = f32[8,16,256]{2,1,0:T(8,128)S(1)} all-to-all(f32[8,16,256]{2,1,0:T(8,128)S(1)} %broadcast_in_dim.13), channel_id=1, replica_groups={{0,8,16,24,32,40,48,56},{1,65,129,193,257,321,385,449},{64,72,80,88,96,..., dimensions={0} | all-to-all | bytes 262144 | tf_op jit(solution)/shard_map/all_to_all | solution.py:214
  48.1 28.8 %reduce-scatter.2.cloned.1.call-done = f32[128,1024]{1,0:T(8,128)} async-done(((f32[1024,1024]{1,0:T(8,128)}), f32[128,1024]{1,0:T(8,128)}) %reduce-scatter.2.cloned.1.call-update) | async-done | bytes 524304 | tf_op jit(solution)/shard_map/reduce_scatter | solution.py:235
  76.8 17.9 %all_to_all.27 = f32[8,16,1024]{2,1,0:T(8,128)S(1)} all-to-all(f32[8,16,1024]{2,1,0:T(8,128)} %bitcast.37), channel_id=1, replica_groups={{0,64,128,192,256,320,384,448},{1,9,17,25,33,41,49,57},{8,72,136,200,26..., dimensions={0} | all-to-all | bytes 1048576 | tf_op jit(solution)/shard_map/all_to_all | solution.py:214
  94.8 15.2 %all_to_all.28 = f32[8,16,1024]{2,1,0:T(8,128)} all-to-all(f32[8,16,1024]{2,1,0:T(8,128)S(1)} %broadcast_in_dim.14), channel_id=1, replica_groups={{0,64,128,192,256,320,384,448},{1,9,17,25,33,41,49,57},{8,72,136,200,26..., dimensions={0} | all-to-all | bytes 1048576 | tf_op jit(solution)/shard_map/all_to_all | solution.py:214
  110.0 0.0 all-gather.2.cloned.1.call-update
  110.0 1.1 broadcast_in_dim.15
  111.1 3.7 %all-to-all-start.4 = ((f32[8,128,256]{2,1,0:T(8,128)}), f32[8,128,256]{2,1,0:T(8,128)S(1)}, u32[]{:S(2)}, u32[]{:S(2)}) async-start(f32[8,128,256]{2,1,0:T(8,128)} %broadcast_in_dim.15), calls=%async_computation.5 | async-start | bytes 2097152 | tf_op jit(solution)/shard_map/all_to_all | solution.py:214
  114.9 0.6 pad_add_fusion.place_ref
  115.5 17.5 %all-to-all-done.4 = f32[8,128,256]{2,1,0:T(8,128)S(1)} async-done(((f32[8,128,256]{2,1,0:T(8,128)}), f32[8,128,256]{2,1,0:T(8,128)S(1)}, u32[]{:S(2)}, u32[]{:S(2)}) %all-to-all-start.4) | async-done | bytes 1048608 | tf_op jit(solution)/shard_map/all_to_all | solution.py:214
  133.0 0.1 bitcast_select_fusion
  133.1 0.1 reverse_select_fusion
  133.2 1.3 copy.9
  134.5 1.7 reshape.35
  136.2 0.0 copy-start.1
  136.2 1.8 convolution_bitcast_fusion
  138.0 2.0 %convolution_multiply_fusion.base_ref = f32[256,1024]{1,0:T(8,128)} fusion(f32[256,256]{1,0:T(8,128)S(1)} %convolution_bitcast_fusion, f32[1024,256]{0,1:T(8,128)S(1)} %reshape.35), kind=kOutput, calls=%fused_computation.1 | convolution fusion | flops 805568512 | bytes 2359296 | tf_op jit(solution)/shard_map/dot_general | solution.py:25
  140.1 20.4 %all-gather.2.cloned.1.call-done.grad_ref = f32[1024,1024]{1,0:T(8,128)} async-done(((f32[128,1024]{1,0:T(8,128)}), f32[1024,1024]{1,0:T(8,128)}) %all-gather.2.cloned.1.call-update) | async-done | bytes 4194320 | tf_op jit(solution)/shard_map/all_gather | solution.py:240
  160.5 0.0 copy-done.1
  160.5 21.1 %shard_map.50 = (f32[16,1024]{1,0:T(8,128)}, f32[16,256]{1,0:T(8,128)}) custom-call(s32[4]{0:T(128)} %pad_add_fusion.place_ref, f32[1024,1024]{1,0:T(8,128)} %all-gather.2.cloned.1.call-done.grad_ref, f32[256,1024]{1,0:T(8,128)} %bitcast.32, f32[256,1024]{1,0:T(8,128)} %convolution_multiply_fusion.base_ref), custom_call_target="tpu_custom_call" | custom-call | tf_op jit(solution)/shard_map/pallas_call | solution.py:173
  (4 shorter events, 0.1 us)
Async XLA Ops:
  7.2 22.1 %copy-start = (bf16[512,1024]{1,0:T(8,128)(2,1)S(1)}, bf16[512,1024]{1,0:T(8,128)(2,1)}, u32[]{:S(2)}) copy-start(bf16[512,1024]{1,0:T(8,128)(2,1)} %param.4) | copy-start | bytes 3145732
  7.2 69.6 %reduce-scatter.2.cloned.1.call-start = ((), (), s32[]{:S(2)}) async-start(), calls=%async_computation.6 | async-start | bytes 4718592 | tf_op jit(solution)/shard_map/reduce_scatter | solution.py:235
  19.9 12.6 %copy-start.2 = (f32[1,16,256]{2,1,0:T(8,128)S(1)}, f32[1,16,256]{2,1,0:T(8,128)}, u32[]{:S(2)}) copy-start(f32[1,16,256]{2,1,0:T(8,128)} %param.5) | copy-start | bytes 49156
  19.9 9.3 %collective-permute-start = (bf16[4,512,128]{1,2,0:T(8,128)(2,1)S(1)}, bf16[4,512,128]{1,2,0:T(8,128)(2,1)S(1)}, u32[]{:S(2)}, u32[]{:S(2)}) collective-permute-start(bf16[4,512,128]{1,2,0:T(8,128)(2,1)S(1)} %all_to_all.25), channel_id=1, source_target_pairs={{0,1},{1,0},{2,3},{3,2},{4,5},{5,4},{6,7},{7,6},{8,9},{9,8},{10,11... | collective-permute-start | bytes 1572872 | tf_op jit(solution)/shard_map/ppermute | solution.py:225
  32.5 128.0 %all-gather.2.cloned.1.call-start = ((), (), s32[]{:S(2)}) async-start(), calls=%async_computation.7 | async-start | bytes 4718592 | tf_op jit(solution)/shard_map/all_gather | solution.py:240
  111.1 21.9 %all-to-all-start.4 = ((f32[8,128,256]{2,1,0:T(8,128)}), f32[8,128,256]{2,1,0:T(8,128)S(1)}, u32[]{:S(2)}, u32[]{:S(2)}) async-start(f32[8,128,256]{2,1,0:T(8,128)} %broadcast_in_dim.15), calls=%async_computation.5 | async-start | bytes 2097152 | tf_op jit(solution)/shard_map/all_to_all | solution.py:214
  136.2 24.3 %copy-start.1 = (f32[1024,256]{0,1:T(8,128)}, f32[1024,256]{0,1:T(8,128)S(1)}, u32[]{:S(2)}) copy-start(f32[1024,256]{0,1:T(8,128)S(1)} %reshape.35) | copy-start | bytes 3145732
Sparse Core Ops, SparseCore 0:
  32.6 44.1 reduce-scatter.1
  110.2 50.2 all-gather.1

commit v6 on v3

--- a/solution.py
+++ b/solution.py
@@ -60,22 +60,49 @@
     return (cross + cross.T) + product((one, two), (one, two), ((1, 1), (0, 0)), NT)
 
 
+def by_halves(left, right):
+    half = RANK // 2
+    return jnp.concatenate(
+        [product([piece[i:i + half] for piece in left], right, THREE) for i in (0, half)]
+    )
+
+
 def inverse_root(matrix, ident, beside=lambda step: None):
     scale = trace(matrix, ident)
     tmat = matrix * (1.0 / scale)
-    zmat = 1.5 * ident - 0.5 * tmat
-    for step in range(1, NS_ITERS):
+    zmat = ident
+    for step in range(NS_ITERS):
         tsp = split(tmat, 2)
-        square = product(tsp, tsp, THREE)
-        beside(step)
-        cube = product(split(square, 2), tsp, THREE)
-        tmat = 2.25 * tmat - 1.5 * square + 0.25 * cube
-        zmat = 1.5 * zmat - 0.5 * product(split(zmat, 2), split(tmat, 2), THREE)
+        last = step == NS_ITERS - 1
+        if not last:
+            square = by_halves(tsp, tsp)
+        if step == 0:
+            zmat = 1.5 * ident - 0.5 * tmat
+        else:
+            zmat = 1.5 * zmat - 0.5 * by_halves(split(zmat, 2), tsp)
+        if not last:
+            cube = by_halves(split(square, 2), tsp)
+            beside(step + 1)
+            tmat = 2.25 * tmat - 1.5 * square + 0.25 * cube
     return zmat * lax.rsqrt(scale)
 
 
 def full_product(left, right):
     return product(split(left, 3), split(right, 3), SIX)
+
+
+def few_rows(left, right):
+    one, two, three = split(left, 3)
+    rows = left.shape[0]
+    first = lax.dot_general(
+        jnp.concatenate([three, two, one]), right[0], NN, preferred_element_type=jnp.float32
+    )
+    second = lax.dot_general(
+        jnp.concatenate([two, one]), right[1], NN, preferred_element_type=jnp.float32
+    )
+    third = lax.dot_general(one, right[2], NN, preferred_element_type=jnp.float32)
+    low = second[:rows] + third + first[:rows]
+    return low + (second[rows:] + first[rows:2 * rows]) + first[2 * rows:]
 
 
 def finish_kernel(
@@ -127,17 +154,24 @@
     prow = rows_ref[inner, :]
     rows_ref[...] = all_ref[:, block].T
     gcol = rows_ref[inner, :]
-    pair = product(split(jnp.concatenate([prow, gcol], axis=0), 3), csp, SIX)
     hmat = product(split(product(csp, split(ritz, 3), SIX), 3), csp, SIX)
     eps = trace(hmat, ident) * (0.1 / RANK)
     hdamp = hmat + eps * ident
-    lead = full_product(pair[:WIDTH], hdamp)
-    rinv = inverse_root(hdamp, ident)
-    last = full_product(jnp.concatenate([lead, pair[WIDTH:]], axis=0), rinv)
+    held = []
+
+    def late(step):
+        if step == 1:
+            held.append(few_rows(jnp.concatenate([prow, gcol], axis=0), csp))
+        if step == 2:
+            held.append(few_rows(held[0][:WIDTH], split(hdamp, 3)))
+
+    rinv = inverse_root(hdamp, ident, late)
+    pair, lead = held
+    last = few_rows(jnp.concatenate([lead, pair[WIDTH:]], axis=0), split(rinv, 3))
     fresh_ref[...] = last[:WIDTH]
     middle = jnp.sqrt(eps) * last[WIDTH:] - pair[WIDTH:]
-    coef = product(split(middle, 3), csp, SIX)
-    update = cols + product(split(coef, 3), psp, SIX)
+    coef = few_rows(middle, csp)
+    update = cols + few_rows(coef, psp)
     for natural in range(8):
         ahead, across = natural // 2, natural % 2
         blocks = [update[:, (4 * side + ahead) * 128:(4 * side + ahead + 1) * 128] for side in (0, 1)]

time: 187 us -> 186 us (level)
  no operation moved by 1% of the time
where the time goes in v6:
time: 186 us; the launch traced here: 184 us
  waiting for transfers between devices  80.4 us (43%)
  blocking collectives  46.3 us (25%)
  Pallas kernels  21.7 us (12%)
  starting transfers between devices  16.2 us (9%)
  between operations  14.2 us (8%)
  matrix products  3.19 us (2%)
    all_to_all x3, blocking collectives, exchange(): lax.all_to_all(parts, axes, split_axis=0, concat_axis=0, tiled=True, axis...  46.3 us
    all_gather x1, waiting for transfers between devices, per_device(): both = lax.all_gather(slab, AXES, axis=0, tiled=True, axis_index_groups=one)  43.2 us
    reduce_scatter x1, waiting for transfers between devices, per_device(): lax.psum_scatter(part, AXES, scatter_dimension=0, tiled=True, axis_index_...  34.9 us
    pallas_call x1, Pallas kernels, finish(): pl.pallas_call(finish_kernel, out_shape=(jax.ShapeDtypeStruct((WIDTH, BLO...  21.7 us
    ppermute x1, starting transfers between devices, per_device(): own_sk = lax.ppermute(own_sk, AXES, sketch_moves())  8.35 us
    ppermute x1, starting transfers between devices, per_device(): far = lax.ppermute(near, 'core', [(0, 1), (1, 0)])  7.81 us
  transfers between devices with their start and end apart: 4, of which 4 were waited for; matrix products, arithmetic and copies ran while one was open for 0% of the time, Pallas kernels for 0%

profile of v6, /device:TPU:1, one launch (start us, length us, event | category | flops | bytes accessed | tf_op | source)
XLA Modules:
  0.0 183.8 jit_solution(13961667471924979453)
XLA Ops:
  7.2 0.0 copy-start
  7.2 0.0 reduce-scatter.2.cloned.1.call-start
  7.2 1.1 copy.5
  8.4 11.6 %all_to_all.15 = bf16[4,512,128]{1,2,0:T(8,128)(2,1)S(1)} all-to-all(bf16[4,512,128]{1,2,0:T(8,128)(2,1)S(1)} %broadcast_in_dim.8), channel_id=1, replica_groups=mesh['z'=8,'y'=8,'x'=4,'core'=2] {'x'}, dimensions={0} | all-to-all | bytes 1048576 | tf_op jit(solution)/shard_map/all_to_all | solution.py:235
  19.9 0.0 copy-start.1
  19.9 7.8 %collective-permute-start = (bf16[4,512,128]{1,2,0:T(8,128)(2,1)S(1)}, bf16[4,512,128]{1,2,0:T(8,128)(2,1)S(1)}, u32[]{:S(2)}, u32[]{:S(2)}) collective-permute-start(bf16[4,512,128]{1,2,0:T(8,128)(2,1)S(1)} %all_to_all.15), channel_id=1, source_target_pairs={{0,1},{1,0},{2,3},{3,2},{4,5},{5,4},{6,7},{7,6},{8,9},{9,8},{10,11... | collective-permute-start | bytes 1572872 | tf_op jit(solution)/shard_map/ppermute | solution.py:246
  27.8 1.5 collective-permute-done
  29.3 0.0 copy-done
  29.3 3.2 %fusion = f32[8,128,1024]{2,1,0:T(8,128)} fusion(bf16[4,512,128]{1,2,0:T(8,128)(2,1)S(1)} %collective-permute-done, bf16[4,512,128]{1,2,0:T(8,128)(2,1)S(1)} %all_to_all.15, bf16[512,1024]{1,0:T(8,128)(2,1)S(1)} %copy-done), kind=kOutput, calls=%fused_computation | convolution fusion | flops 1074266112 | bytes 6291456 | tf_op jit(solution)/shard_map/dot_general | solution.py:248
  32.5 0.0 reduce-scatter.2.cloned.1.call-update
  32.5 0.0 all-gather.2.cloned.1.call-start
  32.5 0.0 copy-done.1
  32.6 8.4 %collective-permute-start.1 = (f32[16,256]{1,0:T(8,128)S(1)}, f32[16,256]{1,0:T(8,128)S(1)}, u32[]{:S(2)}, u32[]{:S(2)}) collective-permute-start(f32[16,256]{1,0:T(8,128)S(1)} %bitcast.19), channel_id=1, source_target_pairs={{0,0},{65,1},{2,2},{67,3},{4,4},{69,5},{6,6},{71,7},{128,8},{73,9}... | collective-permute-start | bytes 49160 | tf_op jit(solution)/shard_map/ppermute | solution.py:257
  40.9 0.8 collective-permute-done.1
  41.8 34.9 %reduce-scatter.2.cloned.1.call-done = f32[128,1024]{1,0:T(8,128)} async-done(((f32[1024,1024]{1,0:T(8,128)}), f32[128,1024]{1,0:T(8,128)}) %reduce-scatter.2.cloned.1.call-update) | async-done | bytes 524304 | tf_op jit(solution)/shard_map/reduce_scatter | solution.py:256
  76.6 18.0 %all_to_all.16 = f32[8,16,1024]{2,1,0:T(8,128)S(1)} all-to-all(f32[8,16,1024]{2,1,0:T(8,128)} %bitcast.17), channel_id=1, replica_groups={{0,64,128,192,256,320,384,448},{1,9,17,25,33,41,49,57},{8,72,136,200,26..., dimensions={0} | all-to-all | bytes 1048576 | tf_op jit(solution)/shard_map/all_to_all | solution.py:235
  94.8 16.6 %all_to_all.17 = f32[8,16,1280]{2,1,0:T(8,128)} all-to-all(f32[8,16,1280]{2,1,0:T(8,128)S(1)} %broadcast_in_dim.9), channel_id=1, replica_groups={{0,64,128,192,256,320,384,448},{1,9,17,25,33,41,49,57},{8,72,136,200,26..., dimensions={0} | all-to-all | bytes 1310720 | tf_op jit(solution)/shard_map/all_to_all | solution.py:235
  111.4 0.0 all-gather.2.cloned.1.call-update
  111.5 0.6 pad_add_fusion.place_ref
  112.1 43.2 %all-gather.2.cloned.1.call-done.both_ref = f32[1024,1280]{1,0:T(8,128)} async-done(((f32[128,1280]{1,0:T(8,128)}), f32[1024,1280]{1,0:T(8,128)}) %all-gather.2.cloned.1.call-update) | async-done | bytes 5242896 | tf_op jit(solution)/shard_map/all_gather | solution.py:262
  155.3 21.7 %shard_map.50 = (f32[16,1024]{1,0:T(8,128)}, f32[16,256]{1,0:T(8,128)}) custom-call(s32[4]{0:T(128)} %pad_add_fusion.place_ref, f32[1024,1280]{1,0:T(8,128)} %all-gather.2.cloned.1.call-done.both_ref), custom_call_target="tpu_custom_call" | custom-call | tf_op jit(solution)/shard_map/pallas_call | solution.py:185
  (4 shorter events, 0.1 us)
Async XLA Ops:
  7.2 22.1 %copy-start = (bf16[512,1024]{1,0:T(8,128)(2,1)S(1)}, bf16[512,1024]{1,0:T(8,128)(2,1)}, u32[]{:S(2)}) copy-start(bf16[512,1024]{1,0:T(8,128)(2,1)} %param.4) | copy-start | bytes 3145732
  7.2 69.5 %reduce-scatter.2.cloned.1.call-start = ((), (), s32[]{:S(2)}) async-start(), calls=%async_computation.4 | async-start | bytes 4718592 | tf_op jit(solution)/shard_map/reduce_scatter | solution.py:256
  19.9 12.6 %copy-start.1 = (f32[1,16,256]{2,1,0:T(8,128)S(1)}, f32[1,16,256]{2,1,0:T(8,128)}, u32[]{:S(2)}) copy-start(f32[1,16,256]{2,1,0:T(8,128)} %param.5) | copy-start | bytes 49156
  19.9 9.3 %collective-permute-start = (bf16[4,512,128]{1,2,0:T(8,128)(2,1)S(1)}, bf16[4,512,128]{1,2,0:T(8,128)(2,1)S(1)}, u32[]{:S(2)}, u32[]{:S(2)}) collective-permute-start(bf16[4,512,128]{1,2,0:T(8,128)(2,1)S(1)} %all_to_all.15), channel_id=1, source_target_pairs={{0,1},{1,0},{2,3},{3,2},{4,5},{5,4},{6,7},{7,6},{8,9},{9,8},{10,11... | collective-permute-start | bytes 1572872 | tf_op jit(solution)/shard_map/ppermute | solution.py:246
  32.5 122.8 %all-gather.2.cloned.1.call-start = ((), (), s32[]{:S(2)}) async-start(), calls=%async_computation.5 | async-start | bytes 5898240 | tf_op jit(solution)/shard_map/all_gather | solution.py:262
  32.6 9.2 %collective-permute-start.1 = (f32[16,256]{1,0:T(8,128)S(1)}, f32[16,256]{1,0:T(8,128)S(1)}, u32[]{:S(2)}, u32[]{:S(2)}) collective-permute-start(f32[16,256]{1,0:T(8,128)S(1)} %bitcast.19), channel_id=1, source_target_pairs={{0,0},{65,1},{2,2},{67,3},{4,4},{69,5},{6,6},{71,7},{128,8},{73,9}... | collective-permute-start | bytes 49160 | tf_op jit(solution)/shard_map/ppermute | solution.py:257
Sparse Core Ops, SparseCore 0:
  32.6 43.9 reduce-scatter.1
  111.6 43.6 all-gather.1

commit v7 on v6

--- a/solution.py
+++ b/solution.py
@@ -255,10 +255,11 @@
     one, two = groups(True), groups(False)
     band = lax.psum_scatter(part, AXES, scatter_dimension=0, tiled=True, axis_index_groups=one)
     own_sk = lax.ppermute(own_sk, AXES, sketch_moves())
+    own_sk = gather(own_sk, AXES, 8, two).reshape(8 * WIDTH, RANK)
     own_sk, band = lax.optimization_barrier((own_sk, band))
     rows = jnp.sum(exchange(band.reshape(8, WIDTH, BLOCK), AXES, two), axis=0)
-    rows = jnp.concatenate([rows, own_sk], axis=1)
-    slab = gather(rows, AXES, 8, two).reshape(8 * WIDTH, BLOCK + RANK)
+    slab = gather(rows, AXES, 8, two).reshape(8 * WIDTH, BLOCK)
+    slab = jnp.concatenate([slab, own_sk], axis=1)
     both = lax.all_gather(slab, AXES, axis=0, tiled=True, axis_index_groups=one)
     z, y = lax.axis_index("z"), lax.axis_index("y")
     places = jnp.stack([z, y, (z % 2 + core) % 2 * 4 + z // 2, core])

time: 186 us -> 186 us (level)
  waiting for transfers between devices: 80.4 us -> 66.5 us
  blocking collectives: 46.3 us -> 59.4 us
    reduce_scatter x1, waiting for transfers between devices: 34.9 us -> 20.6 us  [per_device(): lax.psum_scatter(part, AXES, scatter_dimension=0, tiled=True, axis_index_...]
    all_to_all x3 -> x4, blocking collectives: 46.3 us -> 59.4 us  [exchange(): lax.all_to_all(parts, axes, split_axis=0, concat_axis=0, tiled=True, axis...]
where the time goes in v7:
time: 186 us; the launch traced here: 184 us
  waiting for transfers between devices  66.5 us (36%)
  blocking collectives  59.4 us (32%)
  Pallas kernels  21.7 us (12%)
  starting transfers between devices  16.2 us (9%)
  between operations  14.2 us (8%)
  matrix products  3.19 us (2%)
    all_to_all x4, blocking collectives, exchange(): lax.all_to_all(parts, axes, split_axis=0, concat_axis=0, tiled=True, axis...  59.4 us
    all_gather x1, waiting for transfers between devices, per_device(): both = lax.all_gather(slab, AXES, axis=0, tiled=True, axis_index_groups=one)  43.4 us
    pallas_call x1, Pallas kernels, finish(): pl.pallas_call(finish_kernel, out_shape=(jax.ShapeDtypeStruct((WIDTH, BLO...  21.7 us
    reduce_scatter x1, waiting for transfers between devices, per_device(): lax.psum_scatter(part, AXES, scatter_dimension=0, tiled=True, axis_index_...  20.6 us
    ppermute x1, starting transfers between devices, per_device(): own_sk = lax.ppermute(own_sk, AXES, sketch_moves())  8.35 us
    ppermute x1, starting transfers between devices, per_device(): far = lax.ppermute(near, 'core', [(0, 1), (1, 0)])  7.81 us
  transfers between devices with their start and end apart: 4, of which 4 were waited for; matrix products, arithmetic and copies ran while one was open for 0% of the time, Pallas kernels for 0%

profile of v7, /device:TPU:1, one launch (start us, length us, event | category | flops | bytes accessed | tf_op | source)
XLA Modules:
  0.0 183.9 jit_solution(13608353415965126062)
XLA Ops:
  7.2 0.0 copy-start
  7.2 0.0 reduce-scatter.2.cloned.1.call-start
  7.2 1.1 copy.5
  8.4 11.6 %all_to_all.20 = bf16[4,512,128]{1,2,0:T(8,128)(2,1)S(1)} all-to-all(bf16[4,512,128]{1,2,0:T(8,128)(2,1)S(1)} %broadcast_in_dim.10), channel_id=1, replica_groups=mesh['z'=8,'y'=8,'x'=4,'core'=2] {'x'}, dimensions={0} | all-to-all | bytes 1048576 | tf_op jit(solution)/shard_map/all_to_all | solution.py:235
  19.9 0.0 copy-start.1
  19.9 7.8 %collective-permute-start = (bf16[4,512,128]{1,2,0:T(8,128)(2,1)S(1)}, bf16[4,512,128]{1,2,0:T(8,128)(2,1)S(1)}, u32[]{:S(2)}, u32[]{:S(2)}) collective-permute-start(bf16[4,512,128]{1,2,0:T(8,128)(2,1)S(1)} %all_to_all.20), channel_id=1, source_target_pairs={{0,1},{1,0},{2,3},{3,2},{4,5},{5,4},{6,7},{7,6},{8,9},{9,8},{10,11... | collective-permute-start | bytes 1572872 | tf_op jit(solution)/shard_map/ppermute | solution.py:246
  27.8 1.5 collective-permute-done
  29.3 0.0 copy-done
  29.3 3.2 %fusion = f32[8,128,1024]{2,1,0:T(8,128)} fusion(bf16[4,512,128]{1,2,0:T(8,128)(2,1)S(1)} %collective-permute-done, bf16[4,512,128]{1,2,0:T(8,128)(2,1)S(1)} %all_to_all.20, bf16[512,1024]{1,0:T(8,128)(2,1)S(1)} %copy-done), kind=kOutput, calls=%fused_computation | convolution fusion | flops 1074266112 | bytes 6291456 | tf_op jit(solution)/shard_map/dot_general | solution.py:248
  32.5 0.0 reduce-scatter.2.cloned.1.call-update
  32.5 0.0 all-gather.2.cloned.1.call-start
  32.5 0.0 copy-done.1
  32.6 8.4 %collective-permute-start.1 = (f32[16,256]{1,0:T(8,128)S(1)}, f32[16,256]{1,0:T(8,128)S(1)}, u32[]{:S(2)}, u32[]{:S(2)}) collective-permute-start(f32[16,256]{1,0:T(8,128)S(1)} %bitcast.21), channel_id=1, source_target_pairs={{0,0},{65,1},{2,2},{67,3},{4,4},{69,5},{6,6},{71,7},{128,8},{73,9}... | collective-permute-start | bytes 49160 | tf_op jit(solution)/shard_map/ppermute | solution.py:257
  40.9 0.8 collective-permute-done.1
  41.8 15.3 %all_to_all.21 = f32[8,16,256]{2,1,0:T(8,128)S(1)} all-to-all(f32[8,16,256]{2,1,0:T(8,128)S(1)} %broadcast_in_dim.11), channel_id=1, replica_groups={{0,64,128,192,256,320,384,448},{1,9,17,25,33,41,49,57},{8,72,136,200,26..., dimensions={0} | all-to-all | bytes 262144 | tf_op jit(solution)/shard_map/all_to_all | solution.py:235
  57.1 20.6 %reduce-scatter.2.cloned.1.call-done = f32[128,1024]{1,0:T(8,128)} async-done(((f32[1024,1024]{1,0:T(8,128)}), f32[128,1024]{1,0:T(8,128)}) %reduce-scatter.2.cloned.1.call-update) | async-done | bytes 524304 | tf_op jit(solution)/shard_map/reduce_scatter | solution.py:256
  77.7 18.0 %all_to_all.22 = f32[8,16,1024]{2,1,0:T(8,128)S(1)} all-to-all(f32[8,16,1024]{2,1,0:T(8,128)} %bitcast.19), channel_id=1, replica_groups={{0,64,128,192,256,320,384,448},{1,9,17,25,33,41,49,57},{8,72,136,200,26..., dimensions={0} | all-to-all | bytes 1048576 | tf_op jit(solution)/shard_map/all_to_all | solution.py:235
  95.8 14.5 %all_to_all.23 = f32[8,16,1024]{2,1,0:T(8,128)S(1)} all-to-all(f32[8,16,1024]{2,1,0:T(8,128)S(1)} %broadcast_in_dim.12), channel_id=1, replica_groups={{0,64,128,192,256,320,384,448},{1,9,17,25,33,41,49,57},{8,72,136,200,26..., dimensions={0} | all-to-all | bytes 1048576 | tf_op jit(solution)/shard_map/all_to_all | solution.py:235
  110.3 0.9 pad_maximum_fusion
  111.2 0.0 all-gather.2.cloned.1.call-update
  111.3 0.6 pad_add_fusion.place_ref
  111.9 43.4 %all-gather.2.cloned.1.call-done.both_ref = f32[1024,1280]{1,0:T(8,128)} async-done(((f32[128,1280]{1,0:T(8,128)}), f32[1024,1280]{1,0:T(8,128)}) %all-gather.2.cloned.1.call-update) | async-done | bytes 5242896 | tf_op jit(solution)/shard_map/all_gather | solution.py:263
  155.3 21.7 %shard_map.50 = (f32[16,1024]{1,0:T(8,128)}, f32[16,256]{1,0:T(8,128)}) custom-call(s32[4]{0:T(128)} %pad_add_fusion.place_ref, f32[1024,1280]{1,0:T(8,128)} %all-gather.2.cloned.1.call-done.both_ref), custom_call_target="tpu_custom_call" | custom-call | tf_op jit(solution)/shard_map/pallas_call | solution.py:185
  (4 shorter events, 0.1 us)
Async XLA Ops:
  7.2 22.1 %copy-start = (bf16[512,1024]{1,0:T(8,128)(2,1)S(1)}, bf16[512,1024]{1,0:T(8,128)(2,1)}, u32[]{:S(2)}) copy-start(bf16[512,1024]{1,0:T(8,128)(2,1)} %param.4) | copy-start | bytes 3145732
  7.2 70.5 %reduce-scatter.2.cloned.1.call-start = ((), (), s32[]{:S(2)}) async-start(), calls=%async_computation.5 | async-start | bytes 4718592 | tf_op jit(solution)/shard_map/reduce_scatter | solution.py:256
  19.9 12.6 %copy-start.1 = (f32[1,16,256]{2,1,0:T(8,128)S(1)}, f32[1,16,256]{2,1,0:T(8,128)}, u32[]{:S(2)}) copy-start(f32[1,16,256]{2,1,0:T(8,128)} %param.5) | copy-start | bytes 49156
  19.9 9.3 %collective-permute-start = (bf16[4,512,128]{1,2,0:T(8,128)(2,1)S(1)}, bf16[4,512,128]{1,2,0:T(8,128)(2,1)S(1)}, u32[]{:S(2)}, u32[]{:S(2)}) collective-permute-start(bf16[4,512,128]{1,2,0:T(8,128)(2,1)S(1)} %all_to_all.20), channel_id=1, source_target_pairs={{0,1},{1,0},{2,3},{3,2},{4,5},{5,4},{6,7},{7,6},{8,9},{9,8},{10,11... | collective-permute-start | bytes 1572872 | tf_op jit(solution)/shard_map/ppermute | solution.py:246
  32.5 122.9 %all-gather.2.cloned.1.call-start = ((), (), s32[]{:S(2)}) async-start(), calls=%async_computation.6 | async-start | bytes 5898240 | tf_op jit(solution)/shard_map/all_gather | solution.py:263
  32.6 9.2 %collective-permute-start.1 = (f32[16,256]{1,0:T(8,128)S(1)}, f32[16,256]{1,0:T(8,128)S(1)}, u32[]{:S(2)}, u32[]{:S(2)}) collective-permute-start(f32[16,256]{1,0:T(8,128)S(1)} %bitcast.21), channel_id=1, source_target_pairs={{0,0},{65,1},{2,2},{67,3},{4,4},{69,5},{6,6},{71,7},{128,8},{73,9}... | collective-permute-start | bytes 49160 | tf_op jit(solution)/shard_map/ppermute | solution.py:257
Sparse Core Ops, SparseCore 0:
  32.6 45.0 reduce-scatter.1
  111.4 43.9 all-gather.1
